TPU v7x, 32 devices: a whole 2x2x4 slice. The times are simulated.
32 devices in a mesh: camframe: 16 (over z, x, core), tile: 2 (over y).
Axes of the slice: x: 2, y: 2, z: 4, core: 2. Of those that a mesh axis runs over, the one named last changes fastest.
Arguments:
- latents: bfloat16 [48, 16, 8, 1280], P('camframe', 'tile'), may hold values from -6 to 6
- norm_gain: float32 [1280], replicated, may hold values from 0.1 to 1.9
- norm_shift: float32 [1280], replicated, may hold values from -3 to 3
- conv_weight: bfloat16 [3, 3, 1280, 1280], P(None, None, 'tile'), may hold values from -0.0546875 to 0.0546875
- cross_query: bfloat16 [1280, 1280], P('tile'), may hold values from -1 to 1
- cross_key: bfloat16 [1280, 1280], P('tile'), may hold values from -1 to 1
- cross_value: bfloat16 [1280, 1280], P('tile'), may hold values from -0.15625 to 0.15625
- cross_out: bfloat16 [1280, 1280], P('tile'), may hold values from -0.5 to 0.5
- time_query: bfloat16 [1280, 1280], P('tile'), may hold values from -1 to 1
- time_key: bfloat16 [1280, 1280], P('tile'), may hold values from -1 to 1
- time_value: bfloat16 [1280, 1280], P('tile'), may hold values from -0.15625 to 0.15625
- time_out: bfloat16 [1280, 1280], P('tile'), may hold values from -0.5 to 0.5
- patch_lists: int32 [6, 2, 2], replicated, may hold values from 0 to 3, as said below
- patch_counts: int32 [6, 2], replicated, may hold values from 1 to 2
Outputs:
- blended: bfloat16 [48, 16, 8, 1280], P('camframe', 'tile')
Inputs may be any that keep to these rules, and one draw needn't show every extreme that they name: `patch_lists`: each camera side lists 2 different patch numbers.
All inputs are finite; a program needn't handle non-finite values.
Results may differ from a plain program's by a relative error of at most 0.025.
The roundings to bfloat16 on the way count: a program that leaves them out, or rounds other values in their place, can miss the bound.
Values may be sent and summed in bfloat16 or wider, within the bound.
A program may use at most 128 MiB of HBM per device.

v0:
```python
import jax
import jax.numpy as jnp
from jax import lax
from jax.sharding import PartitionSpec as P

GROUPS = 32
CAMS = 6
HH = 16
WW = 8
PATCH = 32
P_SIZE = 2
HEAD = 160
NPATCH = 4


EPSILON = 1e-05


def for_sending(x):
    return jax.tree.map(lambda a: a.astype(jnp.bfloat16) if a.dtype == jnp.float32 else a, x)


def shifted(block, axis, distance):
    devices = range(lax.axis_size(axis))
    route = [((i - distance) % len(devices), i) for i in devices]
    return lax.ppermute(block, axis, route)


def right_product(left, weight):
    return lax.dot_general(
        left, weight, (((1,), (1,)), ((), ())), preferred_element_type=jnp.float32
    )


def norm_silu(block_views, gain_vector, shift_vector):
    values = block_views.astype(jnp.float32)
    view_count, height, breadth, channels = values.shape
    grouped = values.reshape(view_count, height * breadth, GROUPS, channels // GROUPS)
    average = jnp.mean(grouped, axis=(1, 3), keepdims=True)
    spread = jnp.mean(jnp.square(grouped - average), axis=(1, 3), keepdims=True)
    normed = ((grouped - average) * lax.rsqrt(spread + EPSILON)).reshape(
        view_count, height, breadth, channels
    )
    return jax.nn.silu(normed * gain_vector + shift_vector).astype(jnp.bfloat16)


def convolve(activated, weight):
    view_count, height, breadth, channels = activated.shape
    padded = jnp.pad(activated, ((0, 0), (1, 1), (1, 1), (0, 0)))
    summed = jnp.zeros((view_count * height * breadth, weight.shape[2]), jnp.float32)
    for row_shift in range(3):
        for col_shift in range(3):
            window = padded[
                :, row_shift : row_shift + height, col_shift : col_shift + breadth, :
            ].reshape(-1, channels)
            summed = summed + right_product(window, weight[row_shift, col_shift])
    return summed.reshape(view_count, height, breadth, weight.shape[2])


def layer_norm(values):
    average = jnp.mean(values, axis=-1, keepdims=True)
    spread = jnp.mean(jnp.square(values - average), axis=-1, keepdims=True)
    return ((values - average) * lax.rsqrt(spread + EPSILON)).astype(jnp.bfloat16)


def project(normed, weights):
    flattened = normed.reshape(-1, normed.shape[-1])
    return tuple((right_product(flattened, weight).astype(jnp.bfloat16) for weight in weights))


def attend(queries, key_block, values, live_slots):
    view_count, tokens, channels = queries.shape
    head_count = channels // HEAD
    scores = jnp.einsum(
        "nthd,nlhd->nhtl",
        queries.reshape(view_count, tokens, head_count, HEAD),
        key_block.reshape(view_count, -1, head_count, HEAD),
        preferred_element_type=jnp.float32,
    ) * HEAD ** (-0.5)
    scores = jnp.where(live_slots[:, None, None, :], scores, -jnp.inf)
    highest = jnp.max(scores, axis=-1, keepdims=True)
    weights = jnp.exp(scores - highest)
    weights = (weights / jnp.sum(weights, axis=-1, keepdims=True)).astype(jnp.bfloat16)
    mixture = jnp.einsum(
        "nhtl,nlhd->nthd",
        weights,
        values.reshape(view_count, -1, head_count, HEAD),
        preferred_element_type=jnp.float32,
    )
    return mixture.reshape(view_count, tokens, channels).astype(jnp.bfloat16)


def across_frames(pieces):
    queries, key_block, values = pieces
    view_total, unit_dim, token_count, channels = queries.shape
    head_count = channels // HEAD
    layout = (CAMS, view_total // CAMS, token_count, head_count, HEAD)
    scores = jnp.einsum(
        "cfthd,cgthd->cthfg",
        queries.reshape(layout),
        key_block.reshape(layout),
        preferred_element_type=jnp.float32,
    ) * HEAD ** (-0.5)
    highest = jnp.max(scores, axis=-1, keepdims=True)
    weights = jnp.exp(scores - highest)
    weights = (weights / jnp.sum(weights, axis=-1, keepdims=True)).astype(jnp.bfloat16)
    mixture = jnp.einsum(
        "cthfg,cgthd->cfthd", weights, values.reshape(layout), preferred_element_type=jnp.float32
    )
    return mixture.reshape(view_total, unit_dim, token_count, channels).astype(jnp.bfloat16)


def on_device(
    latents,
    norm_gain,
    norm_shift,
    conv_weight,
    cross_query,
    cross_key,
    cross_value,
    cross_out,
    time_query,
    time_key,
    time_value,
    time_out,
    patch_lists,
    patch_counts,
):
    per_device = latents.shape[0]
    share_rows = latents.shape[1]
    cycle_length = lax.axis_size("camframe")
    cycle_index = lax.axis_index("camframe")
    tile_index = lax.axis_index("tile")
    frames = per_device * cycle_length // CAMS
    tokens = HH * WW
    local_width = conv_weight.shape[2]
    whole_views = lax.all_gather(latents, "tile", axis=1, tiled=True)
    activated = norm_silu(whole_views, norm_gain, norm_shift)
    residual_part = lax.dynamic_slice_in_dim(
        whole_views, tile_index * local_width, local_width, 3
    ).astype(jnp.float32)
    own_hidden = (residual_part + convolve(activated, conv_weight)).astype(jnp.bfloat16)
    hidden = lax.all_gather(own_hidden, "tile", axis=3, tiled=True)
    cross_normed = layer_norm(hidden.astype(jnp.float32))
    cross_queries, cross_keys, cross_values = project(
        cross_normed, (cross_query, cross_key, cross_value)
    )
    cross_queries = cross_queries.reshape(per_device, tokens, local_width)
    packed = jnp.concatenate([cross_keys, cross_values], axis=-1).reshape(
        per_device, NPATCH, PATCH * 2 * local_width
    )
    view_ids = per_device * cycle_index + jnp.arange(per_device, dtype=jnp.int32)
    cameras = view_ids // frames
    picked = {}
    for side_index, step_size in ((0, -frames), (1, frames)):
        offsets = sorted(
            set(((position + step_size) // per_device for position in range(per_device)))
        )
        for offset in offsets:
            targets = [
                position
                for position in range(per_device)
                if (position + step_size) // per_device == offset
            ]
            receiver = (cycle_index - offset) % cycle_length
            chosen = [
                jnp.take(
                    packed[(position + step_size) % per_device],
                    patch_lists[(per_device * receiver + position) // frames, side_index],
                    axis=0,
                )
                for position in targets
            ]
            arrived = shifted(for_sending(jnp.stack(chosen)), "camframe", -offset)
            for order_index, position in enumerate(targets):
                picked[side_index, position] = arrived[order_index]
    context = jnp.stack(
        [
            jnp.concatenate([picked[0, position], picked[1, position]], axis=0)
            for position in range(per_device)
        ]
    )
    context = context.reshape(per_device, 2 * P_SIZE * PATCH, 2 * local_width)
    slot_ids = jnp.arange(P_SIZE, dtype=jnp.int32)
    live_slots = slot_ids[None, None, :] < patch_counts[cameras][:, :, None]
    live_slots = jnp.repeat(live_slots.reshape(per_device, 2 * P_SIZE), PATCH, axis=1)
    cross_mixture = attend(
        cross_queries, context[:, :, :local_width], context[:, :, local_width:], live_slots
    )
    cross_part = jnp.dot(
        cross_mixture.reshape(-1, local_width), cross_out, preferred_element_type=jnp.float32
    ).reshape(per_device, HH, WW, -1)
    combined = lax.psum(cross_part.astype(jnp.bfloat16), "tile").astype(jnp.float32)
    middle = (hidden.astype(jnp.float32) + combined).astype(jnp.bfloat16)
    time_normed = layer_norm(middle.astype(jnp.float32))
    middle_share = lax.dynamic_slice_in_dim(middle, tile_index * share_rows, share_rows, 1)
    time_queries, time_keys, time_values = project(time_normed, (time_query, time_key, time_value))
    block_tokens = tokens // cycle_length
    arranged = tuple(
        (
            part_array.reshape(per_device, cycle_length, block_tokens, local_width)
            for part_array in (time_queries, time_keys, time_values)
        )
    )
    time_mixture = across_frames(
        jax.tree.map(
            lambda part, own: part.astype(own.dtype),
            lax.all_to_all(
                for_sending(arranged), "camframe", split_axis=1, concat_axis=0, tiled=True
            ),
            arranged,
        )
    )
    returned = lax.all_to_all(time_mixture, "camframe", split_axis=0, concat_axis=1, tiled=True)
    row_major = returned.reshape(per_device, HH, WW, local_width).transpose(1, 0, 2, 3)
    row_piece = lax.slice_in_dim(row_major, 0, share_rows * lax.axis_size("tile"), axis=0)
    time_share = lax.psum_scatter(
        jnp.dot(row_piece.reshape(-1, local_width), time_out, preferred_element_type=jnp.float32)
        .reshape(share_rows * lax.axis_size("tile"), per_device, WW, -1)
        .astype(jnp.bfloat16),
        "tile",
        scatter_dimension=0,
        tiled=True,
    ).astype(jnp.float32)
    return (middle_share.astype(jnp.float32) + time_share.transpose(1, 0, 2, 3)).astype(
        jnp.bfloat16
    )


def solution(mesh):
    return jax.shard_map(
        on_device,
        mesh=mesh,
        in_specs=(
            P("camframe", "tile", None, None),
            P(),
            P(),
            P(None, None, "tile", None),
            P("tile", None),
            P("tile", None),
            P("tile", None),
            P("tile", None),
            P("tile", None),
            P("tile", None),
            P("tile", None),
            P("tile", None),
            P(),
            P(),
        ),
        out_specs=P("camframe", "tile", None, None),
        check_vma=False,
    )
```

profile of v0, /device:TPU:0, one launch (start us, length us, event | category | flops | bytes accessed | tf_op | source)
XLA Modules:
  0.0 275.5 jit_solution(16249240783711899736)
XLA Ops:
  7.7 15.1 %all_gather.6 = bf16[3,16,8,1280]{3,2,1,0:T(8,128)(2,1)S(1)} all-gather(bf16[3,8,8,1280]{3,2,1,0:T(8,128)(2,1)} %param.16), channel_id=1, replica_groups=mesh['camframe'=16,'tile'=2] {'tile'}, dimensions={1}, use_global_device_ids=true | all-gather | bytes 1474560 | tf_op jit(solution)/shard_map/all_gather | solution.py:137
  24.8 2.6 pad_slice_fusion.1
  27.4 3.4 %fusion.24 = f32[384,640]{1,0:T(8,128)} fusion(bf16[384,1280]{1,0:T(8,128)(2,1)S(1)} %bitcast.193, bf16[3,3,640,1280]{3,2,1,0:T(8,128)(2,1)} %param.19), kind=kOutput, calls=%fused_computation.48 | convolution fusion | flops 629145600 | bytes 3604480 | tf_op jit(solution)/shard_map/dot_general | solution.py:30
  30.8 3.4 %fusion.28 = f32[384,640]{1,0:T(8,128)} fusion(bf16[384,1280]{1,0:T(8,128)(2,1)S(1)} %bitcast.192, bf16[3,3,640,1280]{3,2,1,0:T(8,128)(2,1)} %param.19), kind=kOutput, calls=%fused_computation.52 | convolution fusion | flops 629145600 | bytes 3604480 | tf_op jit(solution)/shard_map/dot_general | solution.py:30
  34.1 3.4 %fusion.32 = f32[384,640]{1,0:T(8,128)} fusion(bf16[384,1280]{1,0:T(8,128)(2,1)S(1)} %bitcast.178, bf16[3,3,640,1280]{3,2,1,0:T(8,128)(2,1)} %param.19), kind=kOutput, calls=%fused_computation.56 | convolution fusion | flops 629145600 | bytes 3604480 | tf_op jit(solution)/shard_map/dot_general | solution.py:30
  37.5 3.3 %fusion.36 = f32[384,640]{1,0:T(8,128)} fusion(bf16[384,1280]{1,0:T(8,128)(2,1)S(1)} %bitcast.191, bf16[3,3,640,1280]{3,2,1,0:T(8,128)(2,1)} %param.19), kind=kOutput, calls=%fused_computation.60 | convolution fusion | flops 629145600 | bytes 3604480 | tf_op jit(solution)/shard_map/dot_general | solution.py:30
  40.8 3.4 %fusion.38 = f32[384,640]{1,0:T(8,128)} fusion(bf16[384,1280]{1,0:T(8,128)(2,1)S(1)} %bitcast.190, bf16[3,3,640,1280]{3,2,1,0:T(8,128)(2,1)} %param.19), kind=kOutput, calls=%fused_computation.62 | convolution fusion | flops 629145600 | bytes 3604480 | tf_op jit(solution)/shard_map/dot_general | solution.py:30
  44.3 3.4 %fusion.56 = f32[384,640]{1,0:T(8,128)S(1)} fusion(f32[384,640]{1,0:T(8,128)} %fusion.36, f32[384,640]{1,0:T(8,128)} %fusion.38, bf16[384,1280]{1,0:T(8,128)(2,1)} %bitcast.176, bf16[3,3,640,1280]{3,2,1,0:T(8,128)(2,1)} %param.19), kind=kOutput, calls=%fused_computation.79 | convolution fusion | flops 629637120 | bytes 5570560 | tf_op jit(solution)/shard_map/dot_general | solution.py:30
  47.7 2.6 fusion.62
  50.3 2.5 fusion.68
  52.9 2.4 fusion.74
  55.4 13.3 %all_gather.7 = bf16[3,16,8,1280]{3,2,1,0:T(8,128)(2,1)S(1)} all-gather(bf16[3,16,8,640]{3,2,1,0:T(8,128)(2,1)S(1)} %add_convert_fusion), channel_id=1, replica_groups=mesh['camframe'=16,'tile'=2] {'tile'}, dimensions={3}, use_global_device_ids=true | all-gather | bytes 1474560 | tf_op jit(solution)/shard_map/all_gather | solution.py:143
  74.9 1.4 gather_fusion.5
  77.5 1.4 gather_fusion.4
  84.0 1.5 collective-permute-start.3
  85.5 1.2 squeeze.86
  92.7 5.1 %collective-permute-start.1 = (bf16[1,2,40960]{2,1,0:T(2,128)(2,1)}, bf16[1,2,40960]{2,1,0:T(2,128)(2,1)}, u32[]{:S(2)}, u32[]{:S(2)}) collective-permute-start(bf16[1,2,40960]{2,1,0:T(2,128)(2,1)} %fusion.94), channel_id=1, source_target_pairs={{4,0},{6,2},{8,4},{10,6},{12,8},{14,10},{16,12},{18,14},{20,16},{2... | collective-permute-start | bytes 491528 | tf_op jit(solution)/shard_map/ppermute | solution.py:26
  97.8 2.7 convolution_convert_fusion.7
  100.5 1.4 reshape.318
  103.1 1.2 slice_bitcast_fusion.1
  104.4 1.3 pad_maximum_fusion.6
  105.7 1.2 slice_bitcast_fusion.3
  108.2 1.9 copy.67
  111.2 1.3 pad_maximum_fusion.3
  112.9 1.3 pad_maximum_fusion
  115.7 2.1 fusion.81
  117.8 1.7 copy.74
  119.6 1.3 convert_element_type.110
  120.8 2.9 %convolution_convert_fusion.1 = bf16[3,16,8,1280]{3,2,1,0:T(8,128)(2,1)} fusion(bf16[3,16,8,640]{3,2,1,0:T(8,128)(2,1)} %convert_element_type.110, bf16[640,1280]{1,0:T(8,128)(2,1)S(1)} %copy-done), kind=kOutput, calls=%fused_computation.21 | convolution fusion | flops 629637120 | bytes 3112960 | tf_op jit(solution)/shard_map/dot_general | solution.py:190
  123.8 37.2 %all-reduce.3.cloned.1.call-done = bf16[3,16,8,1280]{3,2,1,0:T(8,128)(2,1)} async-done(((bf16[3,16,8,1280]{3,2,1,0:T(8,128)(2,1)}), bf16[3,16,8,1280]{3,2,1,0:T(8,128)(2,1)}) %all-reduce.3.cloned.1.call-update) | async-done | bytes 983056 | tf_op jit(solution)/shard_map/psum | solution.py:193
  161.0 1.6 convert_reduce_fusion.1
  163.3 1.2 copy-done.18
  166.4 5.6 %all-to-all-start = ((bf16[3,16,8,640]{3,2,0,1:T(8,128)(2,1)}), bf16[3,16,8,640]{3,2,0,1:T(8,128)(2,1)S(1)}, u32[]{:S(2)}, u32[]{:S(2)}) async-start(bf16[3,16,8,640]{3,2,0,1:T(8,128)(2,1)} %copy.75), calls=%async_computation | async-start | bytes 983040 | tf_op jit(solution)/shard_map/all_to_all | solution.py:208
  172.0 2.4 convolution_convert_fusion.4
  175.3 10.5 %all-to-all-done = bf16[3,16,8,640]{3,2,0,1:T(8,128)(2,1)S(1)} async-done(((bf16[3,16,8,640]{3,2,0,1:T(8,128)(2,1)}), bf16[3,16,8,640]{3,2,0,1:T(8,128)(2,1)S(1)}, u32[]{:S(2)}, u32[]{:S(2)}) %all-to-all-start) | async-done | bytes 491552 | tf_op jit(solution)/shard_map/all_to_all | solution.py:208
  185.8 4.1 %all-to-all-start.2 = ((bf16[3,16,8,640]{3,2,0,1:T(8,128)(2,1)}), bf16[3,16,8,640]{3,2,0,1:T(8,128)(2,1)S(1)}, u32[]{:S(2)}, u32[]{:S(2)}) async-start(bf16[3,16,8,640]{3,2,0,1:T(8,128)(2,1)} %copy.77), calls=%async_computation.2 | async-start | bytes 983040 | tf_op jit(solution)/shard_map/all_to_all | solution.py:208
  189.9 2.7 convolution_convert_fusion.5
  193.4 10.3 %all-to-all-done.2 = bf16[3,16,8,640]{3,2,0,1:T(8,128)(2,1)S(1)} async-done(((bf16[3,16,8,640]{3,2,0,1:T(8,128)(2,1)}), bf16[3,16,8,640]{3,2,0,1:T(8,128)(2,1)S(1)}, u32[]{:S(2)}, u32[]{:S(2)}) %all-to-all-start.2) | async-done | bytes 491552 | tf_op jit(solution)/shard_map/all_to_all | solution.py:208
  203.7 4.1 %all-to-all-start.1 = ((bf16[3,16,8,640]{3,2,0,1:T(8,128)(2,1)}), bf16[3,16,8,640]{3,2,0,1:T(8,128)(2,1)S(1)}, u32[]{:S(2)}, u32[]{:S(2)}) async-start(bf16[3,16,8,640]{3,2,0,1:T(8,128)(2,1)} %copy.76), calls=%async_computation.1 | async-start | bytes 983040 | tf_op jit(solution)/shard_map/all_to_all | solution.py:208
  208.1 1.4 reshape.237
  209.5 1.4 reshape.241
  210.9 10.6 %all-to-all-done.1 = bf16[3,16,8,640]{3,2,0,1:T(8,128)(2,1)S(1)} async-done(((bf16[3,16,8,640]{3,2,0,1:T(8,128)(2,1)}), bf16[3,16,8,640]{3,2,0,1:T(8,128)(2,1)S(1)}, u32[]{:S(2)}, u32[]{:S(2)}) %all-to-all-start.1) | async-done | bytes 491552 | tf_op jit(solution)/shard_map/all_to_all | solution.py:208
  221.5 1.4 reshape.239
  222.9 2.7 fusion.109
  227.2 17.7 %all_to_all.63 = bf16[48,1,8,640]{3,2,1,0:T(8,128)(2,1)S(1)} all-to-all(bf16[48,1,8,640]{3,2,1,0:T(8,128)(2,1)S(1)} %bitcast.183), channel_id=1, replica_groups=mesh['camframe'=16,'tile'=2] {'camframe'}, dimensions={0} | all-to-all | bytes 983040 | tf_op jit(solution)/shard_map/all_to_all | solution.py:214
  244.9 2.4 convolution_convert_fusion
  248.5 18.2 %reduce-scatter.5.cloned.1.call-done = bf16[8,30720]{1,0:T(8,128)(2,1)} async-done(((bf16[16,30720]{1,0:T(8,128)(2,1)}), bf16[8,30720]{1,0:T(8,128)(2,1)}) %reduce-scatter.5.cloned.1.call-update) | async-done | bytes 491536
  266.7 1.9 fusion.82
  (131 shorter events, 34.3 us)
Async XLA Ops:
  6.5 114.3 %copy-start = (bf16[640,1280]{1,0:T(8,128)(2,1)S(1)}, bf16[640,1280]{1,0:T(8,128)(2,1)}, u32[]{:S(2)}) copy-start(bf16[640,1280]{1,0:T(8,128)(2,1)} %param.23) | copy-start | bytes 4915204
  6.5 154.5 %all-reduce.3.cloned.1.call-start = ((), (), s32[]{:S(2)}) async-start(), calls=%async_computation.5 | async-start | bytes 1966080 | tf_op jit(solution)/shard_map/psum | solution.py:193
  7.7 16.4 %copy-start.13 = (f32[1280]{0:T(1024)S(1)}, f32[1280]{0:T(1024)}, u32[]{:S(2)}) copy-start(f32[1280]{0:T(1024)} %param.18) | copy-start | bytes 15364
  7.7 16.4 %copy-start.14 = (f32[1280]{0:T(1024)S(1)}, f32[1280]{0:T(1024)}, u32[]{:S(2)}) copy-start(f32[1280]{0:T(1024)} %param.17) | copy-start | bytes 15364
  44.3 3.4 %copy-start.5 = (bf16[3,16,8,1280]{3,2,1,0:T(8,128)(2,1)S(1)}, bf16[3,16,8,1280]{3,2,1,0:T(8,128)(2,1)}, u32[]{:S(2)}) copy-start(bf16[3,16,8,1280]{3,2,1,0:T(8,128)(2,1)} %get-tuple-element.22) | copy-start | bytes 2949124
  44.3 3.4 %copy-start.10 = (f32[384,640]{1,0:T(8,128)S(1)}, f32[384,640]{1,0:T(8,128)}, u32[]{:S(2)}) copy-start(f32[384,640]{1,0:T(8,128)} %fusion.32) | copy-start | bytes 2949124
  47.7 2.6 copy-start.4
  47.7 2.6 copy-start.8
  50.3 2.6 copy-start.3
  50.3 2.6 copy-start.7
  68.7 1.4 copy-start.16
  69.6 1.5 copy-start.6
  70.1 1.4 copy-start.17
  81.2 21.9 %collective-permute-start.2 = (bf16[2,2,40960]{2,1,0:T(2,128)(2,1)}, bf16[2,2,40960]{2,1,0:T(2,128)(2,1)}, u32[]{:S(2)}, u32[]{:S(2)}) collective-permute-start(bf16[2,2,40960]{2,1,0:T(2,128)(2,1)} %pad_maximum_fusion.4), channel_id=1, source_target_pairs={{6,0},{8,2},{10,4},{12,6},{14,8},{16,10},{18,12},{20,14},{22,16},{... | collective-permute-start | bytes 983048 | tf_op jit(solution)/shard_map/ppermute | solution.py:26
  84.0 20.4 %collective-permute-start.3 = (bf16[1,2,40960]{2,1,0:T(2,128)(2,1)}, bf16[1,2,40960]{2,1,0:T(2,128)(2,1)}, u32[]{:S(2)}, u32[]{:S(2)}) collective-permute-start(bf16[1,2,40960]{2,1,0:T(2,128)(2,1)} %fusion.97), channel_id=1, source_target_pairs={{28,0},{30,2},{0,4},{2,6},{4,8},{6,10},{8,12},{10,14},{12,16},{14,... | collective-permute-start | bytes 491528 | tf_op jit(solution)/shard_map/ppermute | solution.py:26
  89.9 15.7 %collective-permute-start = (bf16[2,2,40960]{2,1,0:T(2,128)(2,1)}, bf16[2,2,40960]{2,1,0:T(2,128)(2,1)}, u32[]{:S(2)}, u32[]{:S(2)}) collective-permute-start(bf16[2,2,40960]{2,1,0:T(2,128)(2,1)} %pad_maximum_fusion.2), channel_id=1, source_target_pairs={{26,0},{28,2},{30,4},{0,6},{2,8},{4,10},{6,12},{8,14},{10,16},{12,... | collective-permute-start | bytes 983048 | tf_op jit(solution)/shard_map/ppermute | solution.py:26
  92.7 18.5 %collective-permute-start.1 = (bf16[1,2,40960]{2,1,0:T(2,128)(2,1)}, bf16[1,2,40960]{2,1,0:T(2,128)(2,1)}, u32[]{:S(2)}, u32[]{:S(2)}) collective-permute-start(bf16[1,2,40960]{2,1,0:T(2,128)(2,1)} %fusion.94), channel_id=1, source_target_pairs={{4,0},{6,2},{8,4},{10,6},{12,8},{14,10},{16,12},{18,14},{20,16},{2... | collective-permute-start | bytes 491528 | tf_op jit(solution)/shard_map/ppermute | solution.py:26
  97.8 4.1 %copy-start.15 = (s32[6,2]{0,1:T(2,128)S(1)}, s32[6,2]{0,1:T(2,128)}, u32[]{:S(2)}) copy-start(s32[6,2]{0,1:T(2,128)} %param.29) | copy-start | bytes 148
  112.9 2.1 copy-start.11
  162.6 3.0 %copy-start.1 = (bf16[3,16,8,1280]{3,2,1,0:T(8,128)(2,1)}, bf16[3,16,8,1280]{3,2,1,0:T(8,128)(2,1)S(1)}, u32[]{:S(2)}) copy-start(bf16[3,16,8,1280]{3,2,1,0:T(8,128)(2,1)S(1)} %get-tuple-element.13) | copy-start | bytes 2949124
  162.6 2.0 copy-start.18
  163.3 8.7 %copy-start.9 = (bf16[3,16,8,1280]{3,2,1,0:T(8,128)(2,1)}, bf16[3,16,8,1280]{3,2,1,0:T(8,128)(2,1)S(1)}, u32[]{:S(2)}) copy-start(bf16[3,16,8,1280]{3,2,1,0:T(8,128)(2,1)S(1)} %fusion.11) | copy-start | bytes 2949124
  166.4 19.4 %all-to-all-start = ((bf16[3,16,8,640]{3,2,0,1:T(8,128)(2,1)}), bf16[3,16,8,640]{3,2,0,1:T(8,128)(2,1)S(1)}, u32[]{:S(2)}, u32[]{:S(2)}) async-start(bf16[3,16,8,640]{3,2,0,1:T(8,128)(2,1)} %copy.75), calls=%async_computation | async-start | bytes 983040 | tf_op jit(solution)/shard_map/all_to_all | solution.py:208
  185.8 17.9 %all-to-all-start.2 = ((bf16[3,16,8,640]{3,2,0,1:T(8,128)(2,1)}), bf16[3,16,8,640]{3,2,0,1:T(8,128)(2,1)S(1)}, u32[]{:S(2)}, u32[]{:S(2)}) async-start(bf16[3,16,8,640]{3,2,0,1:T(8,128)(2,1)} %copy.77), calls=%async_computation.2 | async-start | bytes 983040 | tf_op jit(solution)/shard_map/all_to_all | solution.py:208
  203.7 17.9 %all-to-all-start.1 = ((bf16[3,16,8,640]{3,2,0,1:T(8,128)(2,1)}), bf16[3,16,8,640]{3,2,0,1:T(8,128)(2,1)S(1)}, u32[]{:S(2)}, u32[]{:S(2)}) async-start(bf16[3,16,8,640]{3,2,0,1:T(8,128)(2,1)} %copy.76), calls=%async_computation.1 | async-start | bytes 983040 | tf_op jit(solution)/shard_map/all_to_all | solution.py:208
  207.8 59.0 %reduce-scatter.5.cloned.1.call-start = ((), (), s32[]{:S(2)}) async-start(), calls=%async_computation.6 | async-start | bytes 1474560
  222.9 2.7 copy-start.12
  247.3 19.4 %copy-start.2 = (bf16[3,16,8,1280]{3,2,1,0:T(8,128)(2,1)S(1)}, bf16[3,16,8,1280]{3,2,1,0:T(8,128)(2,1)}, u32[]{:S(2)}) copy-start(bf16[3,16,8,1280]{3,2,1,0:T(8,128)(2,1)} %copy-done.1) | copy-start | bytes 2949124
Sparse Core Ops, SparseCore 0:
  123.9 37.0 all-reduce.2
  248.6 18.0 reduce-scatter.4
where the time goes:
time: 277 us; the launch traced here: 275 us
  waiting for transfers between devices  86.9 us (31%)
  matrix products  49.7 us (18%)
  blocking collectives  46.1 us (17%)
  local copies, waits for them, and re-layouts  37.1 us (13%)
  starting transfers between devices  22.9 us (8%)
  other arithmetic  18.8 us (7%)
  between operations  14 us (5%)
    dot_general x15, matrix products, right_product(): lax.dot_general(left, weight, (((1,), (1,)), ((), ())), preferred_element...  38.4 us
    psum x1, waiting for transfers between devices, on_device(): lax.psum(cross_part.astype(jnp.bfloat16), 'tile').astype(jnp.float32)  37.2 us
    all_to_all x3, waiting for transfers between devices, on_device(): lax.all_to_all(for_sending(arranged), 'camframe', split_axis=1, concat_ax...  31.4 us
    unnamed x3, waiting for transfers between devices  18.2 us
    all_to_all x1, blocking collectives, on_device(): lax.all_to_all(time_mixture, 'camframe', split_axis=0, concat_axis=1, til...  17.7 us
    all_gather x1, blocking collectives, on_device(): whole_views = lax.all_gather(latents, 'tile', axis=1, tiled=True)  15.1 us
    all_to_all x3, starting transfers between devices, on_device(): lax.all_to_all(for_sending(arranged), 'camframe', split_axis=1, concat_ax...  13.8 us
    all_gather x1, blocking collectives, on_device(): hidden = lax.all_gather(own_hidden, 'tile', axis=3, tiled=True)  13.3 us
  transfers between devices with their start and end apart: 9, of which 5 were waited for; matrix products, arithmetic and copies ran while one was open for 11% of the time, Pallas kernels for 0%

commit v1 on v0

v1 whole, which is shorter than its diff:
```python
import functools

import jax
import jax.numpy as jnp
from jax import lax
from jax.experimental import pallas as pl
from jax.experimental.pallas import tpu as pltpu
from jax.sharding import PartitionSpec as P

GROUPS = 32
CAMS = 6
HH = 16
WW = 8
PATCH = 32
P_SIZE = 2
HEAD = 160
NPATCH = 4
TOKENS = HH * WW

EPSILON = 1e-05
MESH = pl.DeviceIdType.MESH
VMEM_BYTES = 40 * 1024 * 1024


def right_product(left, weight):
    return lax.dot_general(
        left, weight, (((1,), (1,)), ((), ())), preferred_element_type=jnp.float32
    )


def norm_silu(block_views, gain_vector, shift_vector):
    values = block_views.astype(jnp.float32)
    view_count, height, breadth, channels = values.shape
    grouped = values.reshape(view_count, height * breadth, GROUPS, channels // GROUPS)
    average = jnp.mean(grouped, axis=(1, 3), keepdims=True)
    spread = jnp.mean(jnp.square(grouped - average), axis=(1, 3), keepdims=True)
    normed = ((grouped - average) * lax.rsqrt(spread + EPSILON)).reshape(
        view_count, height, breadth, channels
    )
    return jax.nn.silu(normed * gain_vector + shift_vector).astype(jnp.bfloat16)


def convolve(activated, weight):
    return lax.conv_general_dilated(
        activated,
        weight,
        (1, 1),
        ((1, 1), (1, 1)),
        dimension_numbers=("NHWC", "HWOI", "NHWC"),
        preferred_element_type=jnp.float32,
    )


def layer_norm(values):
    average = jnp.mean(values, axis=-1, keepdims=True)
    centred = values - average
    spread = jnp.mean(jnp.square(centred), axis=-1, keepdims=True)
    return (centred * lax.rsqrt(spread + EPSILON)).astype(jnp.bfloat16)


def head_windows(width):
    windows = []
    for head in range(width // HEAD):
        first, last = head * HEAD, (head + 1) * HEAD
        low = first // 128 * 128
        high = min(width, -(-last // 128) * 128)
        windows.append((first, last, low, high))
    return windows


def masked_attention(queries, keys, values, keep, mixture):
    width = queries.shape[1]
    mixture[...] = jnp.zeros_like(mixture)
    for first, last, low, high in head_windows(width):
        lane = lax.broadcasted_iota(jnp.int32, (1, high - low), 1) + low
        inside = (lane >= first) & (lane < last)
        own_queries = jnp.where(inside, queries[:, low:high], jnp.bfloat16(0))
        own_values = jnp.where(inside, values[:, low:high], jnp.bfloat16(0))
        scores = right_product(own_queries, keys[:, low:high]) * HEAD ** (-0.5)
        scores = jnp.where(keep, scores, -jnp.inf)
        highest = jnp.max(scores, axis=-1, keepdims=True)
        weights = jnp.exp(scores - highest)
        weights = (weights / jnp.sum(weights, axis=-1, keepdims=True)).astype(jnp.bfloat16)
        mixture[:, low:high] += jnp.dot(
            weights, own_values, preferred_element_type=jnp.float32
        )
    return mixture[...].astype(jnp.bfloat16)


def cross_kernel(
    cycle, tiles, lists_ref, counts_ref, hidden_ref, wq_ref, wk_ref, wv_ref, wo_ref,
    middle_ref,
    query_buf, kv_buf, send_buf, context, part, arrived, mixture,
    kv_send, kv_recv, rs_send, rs_recv, ag_send, ag_recv,
):
    per_device, _, rows, channels = hidden_ref.shape
    width = wq_ref.shape[0]
    views = per_device * cycle
    frames = views // CAMS
    me = lax.axis_index("camframe")
    tile = lax.axis_index("tile")
    steps = [(side, position, (frames, -frames)[side]) for side in range(2) for position in range(per_device)]
    offsets = sorted({((position + step) // per_device) % cycle for _, position, step in steps})
    barrier = pltpu.get_barrier_semaphore()
    for offset in offsets:
        pl.semaphore_signal(
            barrier, inc=1, device_id=(lax.rem(me + offset, cycle), tile), device_id_type=MESH
        )
    for other in range(1, tiles):
        pl.semaphore_signal(
            barrier, inc=1, device_id=(me, lax.rem(tile + other, tiles)), device_id_type=MESH
        )

    normed = layer_norm(
        hidden_ref[...].reshape(per_device * TOKENS, channels).astype(jnp.float32)
    )
    block = (per_device, NPATCH, PATCH, width)
    kv_buf[:, :, 0] = right_product(normed, wk_ref[...]).astype(jnp.bfloat16).reshape(block)
    kv_buf[:, :, 1] = right_product(normed, wv_ref[...]).astype(jnp.bfloat16).reshape(block)
    pl.semaphore_wait(barrier, len(offsets) + tiles - 1)
    copies = {}
    for side, position, step in steps:
        target_view = lax.rem(per_device * me + position + step + views, views)
        camera = target_view // frames
        for slot in range(P_SIZE):
            chosen = lists_ref[(camera * 2 + side) * P_SIZE + slot]
            send_buf[position, side, slot] = kv_buf[position, chosen]
        target = lax.rem(me + ((position + step) // per_device) % cycle, cycle)
        target_slot = (position + step) % per_device
        copy = pltpu.make_async_remote_copy(
            src_ref=send_buf.at[position, side],
            dst_ref=context.at[target_slot, side],
            send_sem=kv_send.at[position, side],
            recv_sem=kv_recv.at[target_slot, side],
            device_id=(target, tile),
            device_id_type=MESH,
        )
        copy.start()
        copies[target_slot, side] = copy
    query_buf[...] = (
        right_product(normed, wq_ref[...]).astype(jnp.bfloat16).reshape(query_buf.shape)
    )

    def attend(position):
        copies[position, 0].wait_recv()
        copies[position, 1].wait_recv()
        camera = (per_device * me + position) // frames
        place = lax.broadcasted_iota(jnp.int32, (1, 2 * P_SIZE * PATCH), 1) // PATCH
        count = jnp.where(
            place < P_SIZE, counts_ref[camera * 2], counts_ref[camera * 2 + 1]
        )
        keep = lax.rem(place, P_SIZE) < count
        keys = context[position, :, :, 0].reshape(2 * P_SIZE * PATCH, width)
        values = context[position, :, :, 1].reshape(2 * P_SIZE * PATCH, width)
        mixed = masked_attention(query_buf[position], keys, values, keep, mixture)
        total = jnp.dot(mixed, wo_ref[...], preferred_element_type=jnp.float32)
        part[position] = total.astype(jnp.bfloat16).reshape(tiles, rows, channels)
        return scatter(me, tile, tiles, position, part, arrived, rs_send, rs_recv)

    def finish(position, sent):
        total = gather_sum(tile, tiles, position, part, arrived, sent)
        own = hidden_ref[position, tile].astype(jnp.float32) + total
        middle_ref[position, tile] = own.astype(jnp.bfloat16)
        started = []
        for other in range(1, tiles):
            target = lax.rem(tile + other, tiles)
            copy = pltpu.make_async_remote_copy(
                src_ref=middle_ref.at[position, tile],
                dst_ref=middle_ref.at[position, tile],
                send_sem=ag_send.at[position, other],
                recv_sem=ag_recv.at[position, other],
                device_id=(me, target),
                device_id_type=MESH,
            )
            copy.start()
            started.append(copy)
        return started

    pending, started = None, []
    for position in range(per_device):
        sent = attend(position)
        if pending is not None:
            started += finish(*pending)
        pending = (position, sent)
    started += finish(*pending)
    for copy in started:
        copy.wait()
    for copy in copies.values():
        copy.wait_send()


def scatter(me, tile, tiles, position, part, arrived, send_sem, recv_sem):
    started = []
    for other in range(1, tiles):
        target = lax.rem(tile + other, tiles)
        copy = pltpu.make_async_remote_copy(
            src_ref=part.at[position, target],
            dst_ref=arrived.at[position, other],
            send_sem=send_sem.at[position, other],
            recv_sem=recv_sem.at[position, other],
            device_id=(me, target),
            device_id_type=MESH,
        )
        copy.start()
        started.append(copy)
    return started


def gather_sum(tile, tiles, position, part, arrived, sent):
    for copy in sent:
        copy.wait()
    total = part[position, tile].astype(jnp.float32)
    for other in range(1, tiles):
        total = total + arrived[position, other].astype(jnp.float32)
    return total


def time_kernel(
    cycle, tiles, middle_ref, wq_ref, wk_ref, wv_ref, wo_ref,
    out_ref,
    local, received, mixed, returned, part, arrived, mixture,
    qkv_send, qkv_recv, mix_send, mix_recv, rs_send, rs_recv,
):
    per_device, _, rows, channels = middle_ref.shape
    width = wq_ref.shape[0]
    frames = per_device * cycle // CAMS
    cells = TOKENS // frames
    me = lax.axis_index("camframe")
    tile = lax.axis_index("tile")
    first_camera = per_device * me // frames
    last_camera = (per_device * me + per_device - 1) // frames
    reach = (frames - 1 + per_device - 1) // per_device
    barrier = pltpu.get_barrier_semaphore()

    def is_peer(offset):
        other = me + offset
        other_first = (per_device * (other + cycle)) // frames - CAMS
        other_last = (per_device * (other + cycle) + per_device - 1) // frames - CAMS
        return (other >= 0) & (other < cycle) & (other_first <= last_camera) & (first_camera <= other_last)

    for offset in range(-reach, reach + 1):
        if offset != 0:
            @pl.when(is_peer(offset))
            def _():
                pl.semaphore_signal(
                    barrier, inc=1, device_id=(me + offset, tile), device_id_type=MESH
                )
    for other in range(1, tiles):
        pl.semaphore_signal(
            barrier, inc=1, device_id=(me, lax.rem(tile + other, tiles)), device_id_type=MESH
        )

    normed = layer_norm(
        middle_ref[...].reshape(per_device * TOKENS, channels).astype(jnp.float32)
    )
    for which, weight_ref in enumerate((wq_ref, wk_ref, wv_ref)):
        local[:, :, which] = (
            right_product(normed, weight_ref[...])
            .astype(jnp.bfloat16)
            .reshape(per_device, frames, cells, width)
        )
    peers = tiles - 1
    for offset in range(-reach, reach + 1):
        if offset != 0:
            peers = peers + jnp.where(is_peer(offset), 1, 0)
    pl.semaphore_wait(barrier, peers)

    def transpose(source, target, send_sem, recv_sem, slot, group, action):
        unit = per_device * me + slot
        camera, frame = unit // frames, lax.rem(unit, frames)
        goal = camera * frames + group
        goal_device, goal_slot = goal // per_device, lax.rem(goal, per_device)
        remote = pltpu.make_async_remote_copy(
            src_ref=source.at[slot, group],
            dst_ref=target.at[goal_slot, frame],
            send_sem=send_sem.at[slot, group],
            recv_sem=recv_sem.at[goal_slot, frame],
            device_id=(goal_device, tile),
            device_id_type=MESH,
        )
        if action == "start":
            @pl.when(goal_device != me)
            def _():
                remote.start()

            @pl.when(goal_device == me)
            def _():
                pltpu.make_async_copy(
                    source.at[slot, group], target.at[goal_slot, frame], recv_sem.at[goal_slot, frame]
                ).start()
        else:
            @pl.when(goal_device != me)
            def _():
                remote.wait_send()

    def landed(source, target, recv_sem, slot, frame):
        pltpu.make_async_copy(
            source.at[slot, frame], target.at[slot, frame], recv_sem.at[slot, frame]
        ).wait()

    def each(slot, action):
        def body(group, carry):
            action(slot, group)
            return carry

        lax.fori_loop(0, frames, body, 0)

    for slot in range(per_device):
        each(slot, lambda s, g: transpose(local, received, qkv_send, qkv_recv, s, g, "start"))
    tokens_in = frames * cells
    row_cell = lax.rem(lax.broadcasted_iota(jnp.int32, (tokens_in, tokens_in), 0), cells)
    column_cell = lax.rem(lax.broadcasted_iota(jnp.int32, (tokens_in, tokens_in), 1), cells)
    keep = row_cell == column_cell
    for slot in range(per_device):
        each(slot, lambda s, g: landed(local, received, qkv_recv, s, g))
        queries, keys, values = (
            received[slot, :, which].reshape(tokens_in, width) for which in range(3)
        )
        result = masked_attention(queries, keys, values, keep, mixture)
        mixed[slot] = result.reshape(frames, cells, width)
        each(slot, lambda s, g: transpose(mixed, returned, mix_send, mix_recv, s, g, "start"))
    sent = []
    for slot in range(per_device):
        each(slot, lambda s, g: landed(mixed, returned, mix_recv, s, g))
        total = jnp.dot(
            returned[slot].reshape(TOKENS, width), wo_ref[...], preferred_element_type=jnp.float32
        )
        part[slot] = total.astype(jnp.bfloat16).reshape(tiles, rows, channels)
        sent.append(scatter(me, tile, tiles, slot, part, arrived, rs_send, rs_recv))
    for slot in range(per_device):
        total = gather_sum(tile, tiles, slot, part, arrived, sent[slot])
        own = middle_ref[slot, tile].astype(jnp.float32) + total
        out_ref[slot] = own.astype(jnp.bfloat16)
    for slot in range(per_device):
        each(slot, lambda s, g: transpose(local, received, qkv_send, qkv_recv, s, g, "wait"))
        each(slot, lambda s, g: transpose(mixed, returned, mix_send, mix_recv, s, g, "wait"))


def vmem(count):
    return [pl.BlockSpec(memory_space=pltpu.VMEM)] * count


def cross_block(cycle, tiles, lists, counts, hidden, wq, wk, wv, wo):
    per_device, _, rows, channels = hidden.shape
    width = wq.shape[0]
    kind = jnp.bfloat16
    dma = pltpu.SemaphoreType.DMA
    return pl.pallas_call(
        functools.partial(cross_kernel, cycle, tiles),
        out_shape=jax.ShapeDtypeStruct(hidden.shape, kind),
        in_specs=[pl.BlockSpec(memory_space=pltpu.SMEM)] * 2 + vmem(5),
        out_specs=pl.BlockSpec(memory_space=pltpu.VMEM),
        scratch_shapes=[
            pltpu.VMEM((per_device, TOKENS, width), kind),
            pltpu.VMEM((per_device, NPATCH, 2, PATCH, width), kind),
            pltpu.VMEM((per_device, 2, P_SIZE, 2, PATCH, width), kind),
            pltpu.VMEM((per_device, 2, P_SIZE, 2, PATCH, width), kind),
            pltpu.VMEM((per_device, tiles, rows, channels), kind),
            pltpu.VMEM((per_device, tiles, rows, channels), kind),
            pltpu.VMEM((TOKENS, width), jnp.float32),
            dma((per_device, 2)),
            dma((per_device, 2)),
            dma((per_device, tiles)),
            dma((per_device, tiles)),
            dma((per_device, tiles)),
            dma((per_device, tiles)),
        ],
        compiler_params=pltpu.CompilerParams(
            collective_id=1, has_side_effects=True, vmem_limit_bytes=VMEM_BYTES
        ),
        name="cross_block",
    )(lists.reshape(-1), counts.reshape(-1), hidden, wq, wk, wv, wo)


def time_block(cycle, tiles, middle, wq, wk, wv, wo):
    per_device, _, rows, channels = middle.shape
    width = wq.shape[0]
    frames = per_device * cycle // CAMS
    cells = TOKENS // frames
    kind = jnp.bfloat16
    dma = pltpu.SemaphoreType.DMA
    return pl.pallas_call(
        functools.partial(time_kernel, cycle, tiles),
        out_shape=jax.ShapeDtypeStruct((per_device, rows, channels), kind),
        in_specs=vmem(5),
        out_specs=pl.BlockSpec(memory_space=pltpu.VMEM),
        scratch_shapes=[
            pltpu.VMEM((per_device, frames, 3, cells, width), kind),
            pltpu.VMEM((per_device, frames, 3, cells, width), kind),
            pltpu.VMEM((per_device, frames, cells, width), kind),
            pltpu.VMEM((per_device, frames, cells, width), kind),
            pltpu.VMEM((per_device, tiles, rows, channels), kind),
            pltpu.VMEM((per_device, tiles, rows, channels), kind),
            pltpu.VMEM((frames * cells, width), jnp.float32),
            dma((per_device, frames)),
            dma((per_device, frames)),
            dma((per_device, frames)),
            dma((per_device, frames)),
            dma((per_device, tiles)),
            dma((per_device, tiles)),
        ],
        compiler_params=pltpu.CompilerParams(
            collective_id=2, has_side_effects=True, vmem_limit_bytes=VMEM_BYTES
        ),
        name="time_block",
    )(middle, wq, wk, wv, wo)


def on_device(
    latents, norm_gain, norm_shift, conv_weight,
    cross_query, cross_key, cross_value, cross_out,
    time_query, time_key, time_value, time_out,
    patch_lists, patch_counts,
):
    per_device, share_rows = latents.shape[:2]
    channels = latents.shape[3]
    cycle = lax.axis_size("camframe")
    tiles = lax.axis_size("tile")
    tile_index = lax.axis_index("tile")
    local_width = conv_weight.shape[2]
    whole_views = lax.all_gather(latents, "tile", axis=1, tiled=True)
    activated = norm_silu(whole_views, norm_gain, norm_shift)
    residual_part = lax.dynamic_slice_in_dim(
        whole_views, tile_index * local_width, local_width, 3
    ).astype(jnp.float32)
    own_hidden = (residual_part + convolve(activated, conv_weight)).astype(jnp.bfloat16)
    hidden = lax.all_gather(own_hidden, "tile", axis=3, tiled=True)
    hidden = hidden.reshape(per_device, tiles, share_rows * WW, channels)
    middle = cross_block(
        cycle, tiles, patch_lists, patch_counts, hidden,
        cross_query, cross_key, cross_value, cross_out,
    )
    blended = time_block(cycle, tiles, middle, time_query, time_key, time_value, time_out)
    return blended.reshape(latents.shape)


def solution(mesh):
    return jax.shard_map(
        on_device,
        mesh=mesh,
        in_specs=(
            P("camframe", "tile", None, None),
            P(),
            P(),
            P(None, None, "tile", None),
            P("tile", None),
            P("tile", None),
            P("tile", None),
            P("tile", None),
            P("tile", None),
            P("tile", None),
            P("tile", None),
            P("tile", None),
            P(),
            P(),
        ),
        out_specs=P("camframe", "tile", None, None),
        check_vma=False,
    )
```

time: 277 us -> 148 us (0.53)
  Pallas kernels: 0 us -> 89 us
  waiting for transfers between devices: 86.9 us -> 0 us
  local copies, waits for them, and re-layouts: 37.1 us -> 4.33 us
  matrix products: 49.7 us -> 21.1 us
  starting transfers between devices: 22.9 us -> 0 us
  other arithmetic: 18.8 us -> 1.33 us
  blocking collectives: 46.1 us -> 31.8 us
  between operations: 14 us -> 0.22 us
    pallas_call x0 -> x2, Pallas kernels: none -> 89 us  [the longest x1 52.9 us: time_block(): pl.pallas_call(functools.partial(time_kernel, cycle, tiles), out_shape=ja...]
    dot_general x20 -> x0, matrix products: 47 us -> none  [the longest x15 38.4 us: right_product(): lax.dot_general(left, weight, (((1,), (1,)), ((), ())), preferred_element...]
    psum x1 -> x0, waiting for transfers between devices: 37.2 us -> none  [on_device(): lax.psum(cross_part.astype(jnp.bfloat16), 'tile').astype(jnp.float32)]
    all_to_all x3 -> x0, waiting for transfers between devices: 31.4 us -> none  [on_device(): lax.all_to_all(for_sending(arranged), 'camframe', split_axis=1, concat_ax...]
    conv_general_dilated x0 -> x1, matrix products: none -> 21.1 us  [convolve(): lax.conv_general_dilated(activated, weight, (1, 1), ((1, 1), (1, 1)), dim...]
    unnamed x3 -> x0, waiting for transfers between devices: 18.2 us -> none
    all_to_all x1 -> x0, blocking collectives: 17.7 us -> none  [on_device(): lax.all_to_all(time_mixture, 'camframe', split_axis=0, concat_axis=1, til...]
    all_to_all x3 -> x0, starting transfers between devices: 13.8 us -> none  [on_device(): lax.all_to_all(for_sending(arranged), 'camframe', split_axis=1, concat_ax...]
  transfers between devices with their start and end apart: 9 -> 0, of which waited for: 5 -> 0; matrix products, arithmetic and copies ran while one was open for 11% -> 0% of each run, Pallas kernels for 0% -> 0%
where the time goes in v1:
time: 148 us
  Pallas kernels  89 us (60%)
  blocking collectives  31.8 us (21%)
  matrix products  21.1 us (14%)
  local copies, waits for them, and re-layouts  4.33 us (3%)
    pallas_call x1, Pallas kernels, time_block(): pl.pallas_call(functools.partial(time_kernel, cycle, tiles), out_shape=ja...  52.9 us
    pallas_call x1, Pallas kernels, cross_block(): pl.pallas_call(functools.partial(cross_kernel, cycle, tiles), out_shape=j...  36.1 us
    conv_general_dilated x1, matrix products, convolve(): lax.conv_general_dilated(activated, weight, (1, 1), ((1, 1), (1, 1)), dim...  21.1 us
    all_gather x1, blocking collectives, on_device(): hidden = lax.all_gather(own_hidden, 'tile', axis=3, tiled=True)  16.9 us
    all_gather x1, blocking collectives, on_device(): whole_views = lax.all_gather(latents, 'tile', axis=1, tiled=True)  14.9 us
    unnamed x24, local copies, waits for them, and re-layouts  3.44 us

profile of v1, /device:TPU:0, one launch (start us, length us, event | category | flops | bytes accessed | tf_op | source)
XLA Modules:
  0.0 147.8 jit_solution(12467283435980333262)
XLA Ops:
  0.0 0.8 copy.30
  0.8 0.1 reshape.34.counts_ref
  0.8 0.8 copy.29
  1.6 0.1 reshape.33.lists_ref
  1.7 1.1 copy.31
  2.8 14.9 %all_gather.6 = bf16[3,16,8,1280]{3,2,0,1:T(8,128)(2,1)S(1)} all-gather(bf16[3,8,8,1280]{3,2,0,1:T(8,128)(2,1)S(1)} %copy.31), channel_id=1, replica_groups=mesh['camframe'=16,'tile'=2] {'tile'}, dimensions={1}, use_global_device_ids=true | all-gather | bytes 1474560 | tf_op jit(solution)/shard_map/all_gather | solution.py:421
  17.6 0.0 copy-start.8
  17.7 0.0 copy-start.9
  17.7 0.2 convert_reduce_fusion
  17.8 0.1 reduce_sum.24
  17.9 0.1 reduce_sum.25
  18.0 0.1 sub.18
  18.1 0.1 sub.19
  18.2 0.3 fusion.2
  18.5 0.1 reduce_sum.36
  18.6 0.1 reduce_sum.37
  18.7 0.1 mul.29
  18.8 0.1 mul.30
  18.9 0.1 constant_dynamic-slice_fusion
  19.0 0.0 copy-done.8
  19.0 0.0 copy-done.9
  19.0 0.7 fusion.10
  19.7 0.0 copy-start.2
  19.7 0.0 copy-start.3
  19.7 21.1 %fusion.11 = bf16[3,16,8,640]{3,0,2,1:T(4,128)(2,1)S(1)} fusion(bf16[3,3,640,1280]{3,2,1,0:T(8,128)(2,1)} %param.17, bf16[3,16,8,1280]{3,2,0,1:T(8,128)(2,1)S(1)} %fusion.10, bf16[3,16,8,640]{3,2,0,1:T(8,128)(2,1)S(1)} %constant_dynamic-slice_fusion), kind=kOutput, calls=%fused_computation.14 | convolution fusion | flops 4974919680 | bytes 16711680 | tf_op jit(solution)/shard_map/conv_general_dilated | solution.py:44
  40.8 0.0 copy-start
  40.8 0.0 copy-start.1
  40.8 16.9 %all_gather.7 = bf16[3,16,8,1280]{3,0,2,1:T(4,128)(2,1)S(1)} all-gather(bf16[3,16,8,640]{3,0,2,1:T(4,128)(2,1)S(1)} %fusion.11), channel_id=1, replica_groups=mesh['camframe'=16,'tile'=2] {'tile'}, dimensions={3}, use_global_device_ids=true | all-gather | bytes 1474560 | tf_op jit(solution)/shard_map/all_gather | solution.py:427
  57.8 0.1 copy.34
  57.9 0.0 copy-done.2
  57.9 0.0 copy-done.3
  57.9 0.0 copy-done
  57.9 0.0 copy-done.1
  57.9 0.0 copy-start.4
  57.9 0.0 copy-start.5
  57.9 0.0 copy-start.6
  57.9 0.0 copy-start.7
  57.9 36.1 %cross_block.1.middle_ref = bf16[3,2,64,1280]{3,2,1,0:T(8,128)(2,1)S(1)} custom-call(s32[24]{0:T(128)S(1)} %reshape.33.lists_ref, s32[12]{0:T(128)S(1)} %reshape.34.counts_ref, bf16[3,2,64,1280]{3,2,1,0:T(8,128)(2,1)S(1)} %bitcast.3, bf16[640,1280]{1,0:T(8,128)(2,1)S(1)} %copy-done, bf16[640,1280]{1,0:T(8,128)(2,1)S(1)} %copy-done.1, ...), custom_call_target="tpu_custom_call" | custom-call | tf_op jit(solution)/shard_map/cross_block/pallas_call | solution.py:348
  94.1 0.0 copy-done.4
  94.1 0.0 copy-done.5
  94.1 0.0 copy-done.6
  94.1 0.0 copy-done.7
  94.1 52.9 %time_block.1 = bf16[3,64,1280]{2,1,0:T(8,128)(2,1)S(1)} custom-call(bf16[3,2,64,1280]{3,2,1,0:T(8,128)(2,1)S(1)} %cross_block.1.middle_ref, bf16[640,1280]{1,0:T(8,128)(2,1)S(1)} %copy-done.4, bf16[640,1280]{1,0:T(8,128)(2,1)S(1)} %copy-done.5, bf16[640,1280]{1,0:T(8,128)(2,1)S(1)} %copy-done.6, bf16[640,1280]{1,0:T(8,128)(2,1)S(1)} %copy-done.7), custom_call_target="tpu_custom_call" | custom-call | tf_op jit(solution)/shard_map/time_block/pallas_call | solution.py:382
  147.0 0.8 copy.40
  (2 shorter events, 0.0 us)
Async XLA Ops:
  17.6 1.3 copy-start.8
  17.7 1.3 copy-start.9
  19.7 38.2 %copy-start.2 = (bf16[640,1280]{1,0:T(8,128)(2,1)S(1)}, bf16[640,1280]{1,0:T(8,128)(2,1)}, u32[]{:S(2)}) copy-start(bf16[640,1280]{1,0:T(8,128)(2,1)} %wv_ref.2) | copy-start | bytes 4915204
  19.7 38.2 %copy-start.3 = (bf16[640,1280]{1,0:T(8,128)(2,1)S(1)}, bf16[640,1280]{1,0:T(8,128)(2,1)}, u32[]{:S(2)}) copy-start(bf16[640,1280]{1,0:T(8,128)(2,1)} %wo_ref.2) | copy-start | bytes 4915204
  40.8 17.1 %copy-start = (bf16[640,1280]{1,0:T(8,128)(2,1)S(1)}, bf16[640,1280]{1,0:T(8,128)(2,1)}, u32[]{:S(2)}) copy-start(bf16[640,1280]{1,0:T(8,128)(2,1)} %wq_ref.2) | copy-start | bytes 4915204
  40.8 17.1 %copy-start.1 = (bf16[640,1280]{1,0:T(8,128)(2,1)S(1)}, bf16[640,1280]{1,0:T(8,128)(2,1)}, u32[]{:S(2)}) copy-start(bf16[640,1280]{1,0:T(8,128)(2,1)} %wk_ref.2) | copy-start | bytes 4915204
  57.9 36.2 %copy-start.4 = (bf16[640,1280]{1,0:T(8,128)(2,1)S(1)}, bf16[640,1280]{1,0:T(8,128)(2,1)}, u32[]{:S(2)}) copy-start(bf16[640,1280]{1,0:T(8,128)(2,1)} %wq_ref.3) | copy-start | bytes 4915204
  57.9 36.2 %copy-start.5 = (bf16[640,1280]{1,0:T(8,128)(2,1)S(1)}, bf16[640,1280]{1,0:T(8,128)(2,1)}, u32[]{:S(2)}) copy-start(bf16[640,1280]{1,0:T(8,128)(2,1)} %wk_ref.3) | copy-start | bytes 4915204
  57.9 36.2 %copy-start.6 = (bf16[640,1280]{1,0:T(8,128)(2,1)S(1)}, bf16[640,1280]{1,0:T(8,128)(2,1)}, u32[]{:S(2)}) copy-start(bf16[640,1280]{1,0:T(8,128)(2,1)} %wv_ref.3) | copy-start | bytes 4915204
  57.9 36.2 %copy-start.7 = (bf16[640,1280]{1,0:T(8,128)(2,1)S(1)}, bf16[640,1280]{1,0:T(8,128)(2,1)}, u32[]{:S(2)}) copy-start(bf16[640,1280]{1,0:T(8,128)(2,1)} %wo_ref.3) | copy-start | bytes 4915204

commit v2 on v1

--- a/solution.py
+++ b/solution.py
@@ -25,29 +25,6 @@
 def right_product(left, weight):
     return lax.dot_general(
         left, weight, (((1,), (1,)), ((), ())), preferred_element_type=jnp.float32
-    )
-
-
-def norm_silu(block_views, gain_vector, shift_vector):
-    values = block_views.astype(jnp.float32)
-    view_count, height, breadth, channels = values.shape
-    grouped = values.reshape(view_count, height * breadth, GROUPS, channels // GROUPS)
-    average = jnp.mean(grouped, axis=(1, 3), keepdims=True)
-    spread = jnp.mean(jnp.square(grouped - average), axis=(1, 3), keepdims=True)
-    normed = ((grouped - average) * lax.rsqrt(spread + EPSILON)).reshape(
-        view_count, height, breadth, channels
-    )
-    return jax.nn.silu(normed * gain_vector + shift_vector).astype(jnp.bfloat16)
-
-
-def convolve(activated, weight):
-    return lax.conv_general_dilated(
-        activated,
-        weight,
-        (1, 1),
-        ((1, 1), (1, 1)),
-        dimension_numbers=("NHWC", "HWOI", "NHWC"),
-        preferred_element_type=jnp.float32,
     )
 
 
@@ -338,6 +315,169 @@
 
 def vmem(count):
     return [pl.BlockSpec(memory_space=pltpu.VMEM)] * count
+
+
+def group_sums(row, members):
+    high = row.astype(jnp.bfloat16).astype(jnp.float32)
+    middle = (row - high).astype(jnp.bfloat16).astype(jnp.float32)
+    low = row - high - middle
+    place = lax.broadcasted_iota(jnp.int32, (16, row.shape[1]), 0)
+    parts = jnp.where(
+        place == 0, high, jnp.where(place == 1, middle, jnp.where(place == 2, low, 0.0))
+    ).astype(jnp.bfloat16)
+    sums = jnp.dot(parts, members, preferred_element_type=jnp.float32)
+    return jnp.sum(sums, axis=0, keepdims=True)
+
+
+def conv_kernel(
+    tiles, latents_ref, gain_ref, shift_ref, weight_ref,
+    hidden_ref,
+    whole, windows, weights, gathered, total,
+    weight_sem, in_send, in_recv, out_send, out_recv,
+):
+    per_device, rows, channels = latents_ref.shape
+    width = weight_ref.shape[1]
+    me = lax.axis_index("camframe")
+    tile = lax.axis_index("tile")
+    taps = weight_ref.shape[0]
+
+    def load(tap):
+        return pltpu.make_async_copy(weight_ref.at[tap], weights.at[tap], weight_sem.at[tap])
+
+    for tap in range(taps):
+        load(tap).start()
+    barrier = pltpu.get_barrier_semaphore()
+    for other in range(1, tiles):
+        pl.semaphore_signal(
+            barrier, inc=1, device_id=(me, lax.rem(tile + other, tiles)), device_id_type=MESH
+        )
+    pl.semaphore_wait(barrier, tiles - 1)
+
+    def to_others(source, target, send_sem, recv_sem, position):
+        started = []
+        for other in range(1, tiles):
+            copy = pltpu.make_async_remote_copy(
+                src_ref=source,
+                dst_ref=target,
+                send_sem=send_sem.at[position, other],
+                recv_sem=recv_sem.at[position, other],
+                device_id=(me, lax.rem(tile + other, tiles)),
+                device_id_type=MESH,
+            )
+            copy.start()
+            started.append(copy)
+        return started
+
+    incoming = [
+        to_others(
+            latents_ref.at[position], whole.at[position, tile], in_send, in_recv, position
+        )
+        for position in range(per_device)
+    ]
+    size = channels // GROUPS
+    shape = (channels, 128)
+    members = (
+        lax.broadcasted_iota(jnp.int32, shape, 0) // size
+        == lax.broadcasted_iota(jnp.int32, shape, 1)
+    ).astype(jnp.float32).astype(jnp.bfloat16)
+    shape = (128, channels)
+    spread_out = (
+        lax.broadcasted_iota(jnp.int32, shape, 1) // size
+        == lax.broadcasted_iota(jnp.int32, shape, 0)
+    ).astype(jnp.float32).astype(jnp.bfloat16)
+    column = lax.rem(lax.broadcasted_iota(jnp.int32, (TOKENS, 1), 0), WW)
+
+    def group_mean(row):
+        return group_sums(group_sums(row, members) / size, spread_out)
+
+    def prepare(position):
+        whole[position, tile] = latents_ref[position]
+        for copy in incoming[position]:
+            copy.wait()
+        values = whole[position].reshape(TOKENS, channels).astype(jnp.float32)
+        channel_mean = jnp.mean(values, axis=0, keepdims=True)
+        average = group_mean(channel_mean)
+        centred = values - average
+        spread = group_mean(jnp.mean(jnp.square(centred), axis=0, keepdims=True))
+        normed = centred * lax.rsqrt(spread + EPSILON)
+        activated = jax.nn.silu(normed * gain_ref[...] + shift_ref[...])
+        empty_row = jnp.zeros((1, channels), jnp.float32)
+        empty = jnp.zeros((WW, channels), jnp.float32)
+        for col_shift in range(3):
+            if col_shift == 0:
+                moved = jnp.concatenate([empty_row, activated[:-1]], axis=0)
+                moved = jnp.where(column == 0, 0.0, moved)
+            elif col_shift == 2:
+                moved = jnp.concatenate([activated[1:], empty_row], axis=0)
+                moved = jnp.where(column == WW - 1, 0.0, moved)
+            else:
+                moved = activated
+            windows[position, col_shift] = jnp.concatenate(
+                [empty, moved[:-WW]], axis=0
+            ).astype(jnp.bfloat16)
+            windows[position, 3 + col_shift] = moved.astype(jnp.bfloat16)
+            windows[position, 6 + col_shift] = jnp.concatenate(
+                [moved[WW:], empty], axis=0
+            ).astype(jnp.bfloat16)
+
+    outgoing = []
+    for position in range(per_device):
+        prepare(position)
+        total[...] = jnp.zeros_like(total)
+
+        def add(tap, carry):
+            if position == 0:
+                load(tap).wait()
+            total[...] += right_product(windows[position, tap], weights[tap])
+            return carry
+
+        lax.fori_loop(0, taps, add, 0)
+        residual = jnp.zeros((TOKENS, width), jnp.float32)
+        for part in range(tiles):
+            share = whole[position, :, :, part * width : (part + 1) * width]
+            share = share.reshape(TOKENS, width).astype(jnp.float32)
+            residual = jnp.where(tile == part, share, residual)
+        gathered[position, tile] = (residual + total[...]).astype(jnp.bfloat16)
+        outgoing.append(
+            to_others(
+                gathered.at[position, tile], gathered.at[position, tile],
+                out_send, out_recv, position,
+            )
+        )
+    for position in range(per_device):
+        for copy in outgoing[position]:
+            copy.wait()
+        for part in range(tiles):
+            hidden_ref[position, :, part * width : (part + 1) * width] = gathered[position, part]
+
+
+def conv_block(tiles, latents, gain, shift, weight):
+    per_device, rows, channels = latents.shape
+    taps, width = weight.shape[:2]
+    kind = jnp.bfloat16
+    dma = pltpu.SemaphoreType.DMA
+    return pl.pallas_call(
+        functools.partial(conv_kernel, tiles),
+        out_shape=jax.ShapeDtypeStruct((per_device, TOKENS, channels), kind),
+        in_specs=vmem(3) + [pl.BlockSpec(memory_space=pl.ANY)],
+        out_specs=pl.BlockSpec(memory_space=pltpu.VMEM),
+        scratch_shapes=[
+            pltpu.VMEM((per_device, tiles, rows, channels), kind),
+            pltpu.VMEM((per_device, taps, TOKENS, channels), kind),
+            pltpu.VMEM((taps, width, channels), kind),
+            pltpu.VMEM((per_device, tiles, TOKENS, width), kind),
+            pltpu.VMEM((TOKENS, width), jnp.float32),
+            dma((taps,)),
+            dma((per_device, tiles)),
+            dma((per_device, tiles)),
+            dma((per_device, tiles)),
+            dma((per_device, tiles)),
+        ],
+        compiler_params=pltpu.CompilerParams(
+            collective_id=3, has_side_effects=True, vmem_limit_bytes=VMEM_BYTES
+        ),
+        name="conv_block",
+    )(latents, gain, shift, weight)
 
 
 def cross_block(cycle, tiles, lists, counts, hidden, wq, wk, wv, wo):
@@ -416,15 +556,12 @@
     channels = latents.shape[3]
     cycle = lax.axis_size("camframe")
     tiles = lax.axis_size("tile")
-    tile_index = lax.axis_index("tile")
     local_width = conv_weight.shape[2]
-    whole_views = lax.all_gather(latents, "tile", axis=1, tiled=True)
-    activated = norm_silu(whole_views, norm_gain, norm_shift)
-    residual_part = lax.dynamic_slice_in_dim(
-        whole_views, tile_index * local_width, local_width, 3
-    ).astype(jnp.float32)
-    own_hidden = (residual_part + convolve(activated, conv_weight)).astype(jnp.bfloat16)
-    hidden = lax.all_gather(own_hidden, "tile", axis=3, tiled=True)
+    hidden = conv_block(
+        tiles, latents.reshape(per_device, share_rows * WW, channels),
+        norm_gain.reshape(1, channels), norm_shift.reshape(1, channels),
+        conv_weight.reshape(9, local_width, channels),
+    )
     hidden = hidden.reshape(per_device, tiles, share_rows * WW, channels)
     middle = cross_block(
         cycle, tiles, patch_lists, patch_counts, hidden,

time: 148 us -> 130 us (0.88)
  Pallas kernels: 89 us -> 124 us
  blocking collectives: 31.8 us -> 0 us
  matrix products: 21.1 us -> 0 us
    pallas_call x0 -> x1, Pallas kernels: none -> 35.2 us  [conv_block(): pl.pallas_call(functools.partial(conv_kernel, tiles), out_shape=jax.Shape...]
    all_gather x2 -> x0, blocking collectives: 31.8 us -> none  [the longest x1 16.9 us: on_device(): hidden = lax.all_gather(own_hidden, 'tile', axis=3, tiled=True)]
    conv_general_dilated x1 -> x0, matrix products: 21.1 us -> none  [convolve(): lax.conv_general_dilated(activated, weight, (1, 1), ((1, 1), (1, 1)), dim...]
    unnamed x24 -> x21, local copies, waits for them, and re-layouts: 3.44 us -> 3.38 us
where the time goes in v2:
time: 130 us; the launch traced here: 129 us
  Pallas kernels  124 us (95%)
  local copies, waits for them, and re-layouts  4.96 us (4%)
    pallas_call x1, Pallas kernels, time_block(): pl.pallas_call(functools.partial(time_kernel, cycle, tiles), out_shape=ja...  52.6 us
    pallas_call x1, Pallas kernels, cross_block(): pl.pallas_call(functools.partial(cross_kernel, cycle, tiles), out_shape=j...  36.6 us
    pallas_call x1, Pallas kernels, conv_block(): pl.pallas_call(functools.partial(conv_kernel, tiles), out_shape=jax.Shape...  35.2 us
    unnamed x21, local copies, waits for them, and re-layouts  3.38 us

profile of v2, /device:TPU:0, one launch (start us, length us, event | category | flops | bytes accessed | tf_op | source)
XLA Modules:
  0.0 129.4 jit_solution(5474238535779915250)
XLA Ops:
  0.0 0.8 copy.18
  0.8 0.1 reshape.25.counts_ref
  0.8 0.7 reshape.27.gain_ref
  1.5 0.7 reshape.28.shift_ref
  2.2 0.8 copy.17
  3.0 0.1 reshape.24.lists_ref
  3.1 0.0 copy-start.8
  3.1 1.0 copy-done.8
  4.1 0.0 copy-start
  4.2 0.0 copy-start.1
  4.2 0.0 copy-start.2
  4.2 0.0 copy-start.3
  4.2 35.2 %conv_block.1 = bf16[3,128,1280]{2,1,0:T(8,128)(2,1)S(1)} custom-call(bf16[3,64,1280]{2,1,0:T(8,128)(2,1)S(1)} %bitcast.6, f32[1,1280]{1,0:T(1,128)S(1)} %reshape.27.gain_ref, f32[1,1280]{1,0:T(1,128)S(1)} %reshape.28.shift_ref, bf16[9,640,1280]{2,1,0:T(8,128)(2,1)} %bitcast.7), custom_call_target="tpu_custom_call" | custom-call | tf_op jit(solution)/shard_map/conv_block/pallas_call | solution.py:459
  39.3 0.0 copy-done
  39.3 0.0 copy-done.1
  39.4 0.0 copy-done.2
  39.4 0.0 copy-done.3
  39.4 0.0 copy-start.4
  39.4 0.0 copy-start.5
  39.4 0.0 copy-start.6
  39.4 0.0 copy-start.7
  39.4 36.6 %cross_block.1.middle_ref = bf16[3,2,64,1280]{3,2,1,0:T(8,128)(2,1)S(1)} custom-call(s32[24]{0:T(128)S(1)} %reshape.24.lists_ref, s32[12]{0:T(128)S(1)} %reshape.25.counts_ref, bf16[3,2,64,1280]{3,2,1,0:T(8,128)(2,1)S(1)} %bitcast.4, bf16[640,1280]{1,0:T(8,128)(2,1)S(1)} %copy-done, bf16[640,1280]{1,0:T(8,128)(2,1)S(1)} %copy-done.1, ...), custom_call_target="tpu_custom_call" | custom-call | tf_op jit(solution)/shard_map/cross_block/pallas_call | solution.py:488
  76.0 0.0 copy-done.4
  76.0 0.0 copy-done.5
  76.0 0.0 copy-done.6
  76.0 0.0 copy-done.7
  76.0 52.6 %time_block.1 = bf16[3,64,1280]{2,1,0:T(8,128)(2,1)S(1)} custom-call(bf16[3,2,64,1280]{3,2,1,0:T(8,128)(2,1)S(1)} %cross_block.1.middle_ref, bf16[640,1280]{1,0:T(8,128)(2,1)S(1)} %copy-done.4, bf16[640,1280]{1,0:T(8,128)(2,1)S(1)} %copy-done.5, bf16[640,1280]{1,0:T(8,128)(2,1)S(1)} %copy-done.6, bf16[640,1280]{1,0:T(8,128)(2,1)S(1)} %copy-done.7), custom_call_target="tpu_custom_call" | custom-call | tf_op jit(solution)/shard_map/time_block/pallas_call | solution.py:522
  128.6 0.8 copy.20
Async XLA Ops:
  3.1 1.0 copy-start.8
  4.1 35.2 %copy-start = (bf16[640,1280]{1,0:T(8,128)(2,1)S(1)}, bf16[640,1280]{1,0:T(8,128)(2,1)}, u32[]{:S(2)}) copy-start(bf16[640,1280]{1,0:T(8,128)(2,1)} %wq_ref.2) | copy-start | bytes 4915204
  4.2 35.2 %copy-start.1 = (bf16[640,1280]{1,0:T(8,128)(2,1)S(1)}, bf16[640,1280]{1,0:T(8,128)(2,1)}, u32[]{:S(2)}) copy-start(bf16[640,1280]{1,0:T(8,128)(2,1)} %wk_ref.2) | copy-start | bytes 4915204
  4.2 35.2 %copy-start.2 = (bf16[640,1280]{1,0:T(8,128)(2,1)S(1)}, bf16[640,1280]{1,0:T(8,128)(2,1)}, u32[]{:S(2)}) copy-start(bf16[640,1280]{1,0:T(8,128)(2,1)} %wv_ref.2) | copy-start | bytes 4915204
  4.2 35.2 %copy-start.3 = (bf16[640,1280]{1,0:T(8,128)(2,1)S(1)}, bf16[640,1280]{1,0:T(8,128)(2,1)}, u32[]{:S(2)}) copy-start(bf16[640,1280]{1,0:T(8,128)(2,1)} %wo_ref.2) | copy-start | bytes 4915204
  39.4 36.6 %copy-start.4 = (bf16[640,1280]{1,0:T(8,128)(2,1)S(1)}, bf16[640,1280]{1,0:T(8,128)(2,1)}, u32[]{:S(2)}) copy-start(bf16[640,1280]{1,0:T(8,128)(2,1)} %wq_ref.3) | copy-start | bytes 4915204
  39.4 36.6 %copy-start.5 = (bf16[640,1280]{1,0:T(8,128)(2,1)S(1)}, bf16[640,1280]{1,0:T(8,128)(2,1)}, u32[]{:S(2)}) copy-start(bf16[640,1280]{1,0:T(8,128)(2,1)} %wk_ref.3) | copy-start | bytes 4915204
  39.4 36.6 %copy-start.6 = (bf16[640,1280]{1,0:T(8,128)(2,1)S(1)}, bf16[640,1280]{1,0:T(8,128)(2,1)}, u32[]{:S(2)}) copy-start(bf16[640,1280]{1,0:T(8,128)(2,1)} %wv_ref.3) | copy-start | bytes 4915204
  39.4 36.6 %copy-start.7 = (bf16[640,1280]{1,0:T(8,128)(2,1)S(1)}, bf16[640,1280]{1,0:T(8,128)(2,1)}, u32[]{:S(2)}) copy-start(bf16[640,1280]{1,0:T(8,128)(2,1)} %wo_ref.3) | copy-start | bytes 4915204

commit v3 on v1

v3 whole, which is shorter than its diff:
```python
import functools

import jax
import jax.numpy as jnp
from jax import lax
from jax.experimental import pallas as pl
from jax.experimental.pallas import tpu as pltpu
from jax.sharding import PartitionSpec as P

GROUPS = 32
CAMS = 6
HH = 16
WW = 8
PATCH = 32
P_SIZE = 2
HEAD = 160
NPATCH = 4
TOKENS = HH * WW

EPSILON = 1e-05
MESH = pl.DeviceIdType.MESH
VMEM_BYTES = 58 * 1024 * 1024


def right_product(left, weight):
    return lax.dot_general(
        left, weight, (((1,), (1,)), ((), ())), preferred_element_type=jnp.float32
    )


def layer_norm(values):
    average = jnp.mean(values, axis=-1, keepdims=True)
    centred = values - average
    spread = jnp.mean(jnp.square(centred), axis=-1, keepdims=True)
    return (centred * lax.rsqrt(spread + EPSILON)).astype(jnp.bfloat16)


def head_windows(width):
    windows = []
    for head in range(width // HEAD):
        first, last = head * HEAD, (head + 1) * HEAD
        low = first // 128 * 128
        high = min(width, -(-last // 128) * 128)
        windows.append((first, last, low, high))
    return windows


def masked_attention(queries, keys, values, keep, mixture):
    width = queries.shape[1]
    mixture[...] = jnp.zeros_like(mixture)
    for first, last, low, high in head_windows(width):
        lane = lax.broadcasted_iota(jnp.int32, (1, high - low), 1) + low
        inside = (lane >= first) & (lane < last)
        own_queries = jnp.where(inside, queries[:, low:high], jnp.bfloat16(0))
        own_values = jnp.where(inside, values[:, low:high], jnp.bfloat16(0))
        scores = right_product(own_queries, keys[:, low:high]) * HEAD ** (-0.5)
        scores = jnp.where(keep, scores, -jnp.inf)
        highest = jnp.max(scores, axis=-1, keepdims=True)
        weights = jnp.exp(scores - highest)
        weights = (weights / jnp.sum(weights, axis=-1, keepdims=True)).astype(jnp.bfloat16)
        mixture[:, low:high] += jnp.dot(
            weights, own_values, preferred_element_type=jnp.float32
        )
    return mixture[...].astype(jnp.bfloat16)


def group_sums(row, members):
    high = row.astype(jnp.bfloat16).astype(jnp.float32)
    middle = (row - high).astype(jnp.bfloat16).astype(jnp.float32)
    low = row - high - middle
    place = lax.broadcasted_iota(jnp.int32, (16, row.shape[1]), 0)
    parts = jnp.where(
        place == 0, high, jnp.where(place == 1, middle, jnp.where(place == 2, low, 0.0))
    ).astype(jnp.bfloat16)
    sums = jnp.dot(parts, members, preferred_element_type=jnp.float32)
    return jnp.sum(sums, axis=0, keepdims=True)


def scatter(me, tile, tiles, position, part, arrived, send_sem, recv_sem):
    started = []
    for other in range(1, tiles):
        target = lax.rem(tile + other, tiles)
        copy = pltpu.make_async_remote_copy(
            src_ref=part.at[position, target],
            dst_ref=arrived.at[position, other],
            send_sem=send_sem.at[position, other],
            recv_sem=recv_sem.at[position, other],
            device_id=(me, target),
            device_id_type=MESH,
        )
        copy.start()
        started.append(copy)
    return started


def gather_sum(tile, tiles, position, part, arrived, sent):
    for copy in sent:
        copy.wait()
    total = part[position, tile].astype(jnp.float32)
    for other in range(1, tiles):
        total = total + arrived[position, other].astype(jnp.float32)
    return total


def block_kernel(
    cycle, tiles, lists_ref, counts_ref, latents_ref, gain_ref, shift_ref, conv_ref,
    cq_ref, ck_ref, cv_ref, co_ref, tq_ref, tk_ref, tv_ref, to_ref,
    out_ref,
    whole, windows, conv_weights, gathered, total, matrices,
    query_buf, kv_buf, send_buf, context, part, arrived, mixture, middle,
    local, received, mixed, returned, time_part, time_arrived,
    conv_sem, matrix_sem, in_send, in_recv, out_send, out_recv,
    kv_send, kv_recv, rs_send, rs_recv, ag_send, ag_recv,
    qkv_send, qkv_recv, mix_send, mix_recv, rt_send, rt_recv,
):
    per_device, rows, channels = latents_ref.shape
    taps, width = conv_ref.shape[:2]
    views = per_device * cycle
    frames = views // CAMS
    cells = TOKENS // frames
    me = lax.axis_index("camframe")
    tile = lax.axis_index("tile")

    def load(tap):
        return pltpu.make_async_copy(
            conv_ref.at[tap], conv_weights.at[tap], conv_sem.at[tap]
        )

    loads = [
        pltpu.make_async_copy(ref, matrices.at[index], matrix_sem.at[index])
        for index, ref in enumerate(
            (cq_ref, ck_ref, cv_ref, co_ref, tq_ref, tk_ref, tv_ref, to_ref)
        )
    ]
    loaded = set()

    def matrix(index):
        if index not in loaded:
            loads[index].wait()
            loaded.add(index)
        return matrices[index]

    for tap in range(taps):
        load(tap).start()
    steps = [
        (side, position, (frames, -frames)[side])
        for side in range(2)
        for position in range(per_device)
    ]
    offsets = sorted({((position + step) // per_device) % cycle for _, position, step in steps})
    first_camera = per_device * me // frames
    last_camera = (per_device * me + per_device - 1) // frames
    reach = (frames - 1 + per_device - 1) // per_device
    barrier = pltpu.get_barrier_semaphore()

    def is_peer(offset):
        other = me + offset
        other_first = (per_device * (other + cycle)) // frames - CAMS
        other_last = (per_device * (other + cycle) + per_device - 1) // frames - CAMS
        return (other >= 0) & (other < cycle) & (other_first <= last_camera) & (first_camera <= other_last)

    peers = len(offsets) + tiles - 1
    for offset in offsets:
        pl.semaphore_signal(
            barrier, inc=1, device_id=(lax.rem(me + offset, cycle), tile), device_id_type=MESH
        )
    for offset in range(-reach, reach + 1):
        if offset != 0:
            peers = peers + jnp.where(is_peer(offset), 1, 0)

            @pl.when(is_peer(offset))
            def _():
                pl.semaphore_signal(
                    barrier, inc=1, device_id=(me + offset, tile), device_id_type=MESH
                )
    for other in range(1, tiles):
        pl.semaphore_signal(
            barrier, inc=1, device_id=(me, lax.rem(tile + other, tiles)), device_id_type=MESH
        )
    pl.semaphore_wait(barrier, peers)

    def to_others(source, target, send_sem, recv_sem, position):
        started = []
        for other in range(1, tiles):
            copy = pltpu.make_async_remote_copy(
                src_ref=source,
                dst_ref=target,
                send_sem=send_sem.at[position, other],
                recv_sem=recv_sem.at[position, other],
                device_id=(me, lax.rem(tile + other, tiles)),
                device_id_type=MESH,
            )
            copy.start()
            started.append(copy)
        return started

    incoming = [
        to_others(
            latents_ref.at[position], whole.at[position, tile], in_send, in_recv, position
        )
        for position in range(per_device)
    ]
    for copy in loads:
        copy.start()
    size = channels // GROUPS
    shape = (channels, 128)
    members = (
        lax.broadcasted_iota(jnp.int32, shape, 0) // size
        == lax.broadcasted_iota(jnp.int32, shape, 1)
    ).astype(jnp.float32).astype(jnp.bfloat16)
    shape = (128, channels)
    spread_out = (
        lax.broadcasted_iota(jnp.int32, shape, 1) // size
        == lax.broadcasted_iota(jnp.int32, shape, 0)
    ).astype(jnp.float32).astype(jnp.bfloat16)
    column = lax.rem(lax.broadcasted_iota(jnp.int32, (TOKENS, 1), 0), WW)

    def group_mean(row):
        return group_sums(group_sums(row, members) / size, spread_out)

    def prepare(position):
        whole[position, tile] = latents_ref[position]
        for copy in incoming[position]:
            copy.wait()
        values = whole[position].reshape(TOKENS, channels).astype(jnp.float32)
        channel_mean = jnp.mean(values, axis=0, keepdims=True)
        average = group_mean(channel_mean)
        centred = values - average
        spread = group_mean(jnp.mean(jnp.square(centred), axis=0, keepdims=True))
        normed = centred * lax.rsqrt(spread + EPSILON)
        activated = jax.nn.silu(normed * gain_ref[...].reshape(1, channels) + shift_ref[...].reshape(1, channels))
        empty_row = jnp.zeros((1, channels), jnp.float32)
        empty = jnp.zeros((WW, channels), jnp.float32)
        for col_shift in range(3):
            if col_shift == 0:
                moved = jnp.concatenate([empty_row, activated[:-1]], axis=0)
                moved = jnp.where(column == 0, 0.0, moved)
            elif col_shift == 2:
                moved = jnp.concatenate([activated[1:], empty_row], axis=0)
                moved = jnp.where(column == WW - 1, 0.0, moved)
            else:
                moved = activated
            windows[col_shift] = jnp.concatenate(
                [empty, moved[:-WW]], axis=0
            ).astype(jnp.bfloat16)
            windows[3 + col_shift] = moved.astype(jnp.bfloat16)
            windows[6 + col_shift] = jnp.concatenate(
                [moved[WW:], empty], axis=0
            ).astype(jnp.bfloat16)

    def convolve(position):
        prepare(position)
        total[...] = jnp.zeros_like(total)

        def add(tap, carry):
            if position == 0:
                load(tap).wait()
            total[...] += right_product(windows[tap], conv_weights[tap])
            return carry

        lax.fori_loop(0, taps, add, 0)
        residual = jnp.zeros((TOKENS, width), jnp.float32)
        for piece in range(tiles):
            share = whole[position, :, :, piece * width : (piece + 1) * width]
            share = share.reshape(TOKENS, width).astype(jnp.float32)
            residual = jnp.where(tile == piece, share, residual)
        gathered[position, tile] = (residual + total[...]).astype(jnp.bfloat16)
        return to_others(
            gathered.at[position, tile], gathered.at[position, tile],
            out_send, out_recv, position,
        )

    copies = {}

    def share_context(position, outgoing):
        for copy in outgoing:
            copy.wait()
        for piece in range(tiles):
            whole[position, :, :, piece * width : (piece + 1) * width] = gathered[
                position, piece
            ].reshape(tiles, rows, width)
        normed = layer_norm(whole[position].reshape(TOKENS, channels).astype(jnp.float32))
        block = (NPATCH, PATCH, width)
        for which in range(2):
            kv_buf[position, :, which] = (
                right_product(normed, matrix(1 + which)).astype(jnp.bfloat16).reshape(block)
            )
        for side in range(2):
            step = (frames, -frames)[side]
            target_view = lax.rem(per_device * me + position + step + views, views)
            camera = target_view // frames
            for slot in range(P_SIZE):
                chosen = lists_ref[camera, side, slot]
                send_buf[position, side, slot] = kv_buf[position, chosen]
            target = lax.rem(me + ((position + step) // per_device) % cycle, cycle)
            target_slot = (position + step) % per_device
            copy = pltpu.make_async_remote_copy(
                src_ref=send_buf.at[position, side],
                dst_ref=context.at[target_slot, side],
                send_sem=kv_send.at[position, side],
                recv_sem=kv_recv.at[target_slot, side],
                device_id=(target, tile),
                device_id_type=MESH,
            )
            copy.start()
            copies[target_slot, side] = copy
        query_buf[position] = right_product(normed, matrix(0)).astype(jnp.bfloat16)

    pending = None
    for position in range(per_device):
        outgoing = convolve(position)
        if pending is not None:
            share_context(*pending)
        pending = (position, outgoing)
    share_context(*pending)

    def attend(position):
        copies[position, 0].wait_recv()
        copies[position, 1].wait_recv()
        camera = (per_device * me + position) // frames
        place = lax.broadcasted_iota(jnp.int32, (1, 2 * P_SIZE * PATCH), 1) // PATCH
        count = jnp.where(place < P_SIZE, counts_ref[camera, 0], counts_ref[camera, 1])
        live = lax.rem(place, P_SIZE) < count
        keys = context[position, :, :, 0].reshape(2 * P_SIZE * PATCH, width)
        values = context[position, :, :, 1].reshape(2 * P_SIZE * PATCH, width)
        result = masked_attention(query_buf[position], keys, values, live, mixture)
        product = jnp.dot(result, matrix(3), preferred_element_type=jnp.float32)
        part[position] = product.astype(jnp.bfloat16).reshape(tiles, rows, channels)
        return scatter(me, tile, tiles, position, part, arrived, rs_send, rs_recv)

    def finish(position, sent):
        added = gather_sum(tile, tiles, position, part, arrived, sent)
        own = whole[position, tile].astype(jnp.float32) + added
        middle[position, tile] = own.astype(jnp.bfloat16)
        return to_others(
            middle.at[position, tile], middle.at[position, tile], ag_send, ag_recv, position
        )

    def transpose(source, target, send_sem, recv_sem, slot, group, action):
        unit = per_device * me + slot
        camera, frame = unit // frames, lax.rem(unit, frames)
        goal = camera * frames + group
        goal_device, goal_slot = goal // per_device, lax.rem(goal, per_device)
        remote = pltpu.make_async_remote_copy(
            src_ref=source.at[slot, group],
            dst_ref=target.at[goal_slot, frame],
            send_sem=send_sem.at[slot, group],
            recv_sem=recv_sem.at[goal_slot, frame],
            device_id=(goal_device, tile),
            device_id_type=MESH,
        )
        if action == "start":
            @pl.when(goal_device != me)
            def _():
                remote.start()

            @pl.when(goal_device == me)
            def _():
                pltpu.make_async_copy(
                    source.at[slot, group], target.at[goal_slot, frame], recv_sem.at[goal_slot, frame]
                ).start()
        else:
            @pl.when(goal_device != me)
            def _():
                remote.wait_send()

    def landed(source, target, recv_sem, slot, frame):
        pltpu.make_async_copy(
            source.at[slot, frame], target.at[slot, frame], recv_sem.at[slot, frame]
        ).wait()

    def each(slot, action):
        def body(group, carry):
            action(slot, group)
            return carry

        lax.fori_loop(0, frames, body, 0)

    def share_frames(position, outgoing):
        for copy in outgoing:
            copy.wait()
        normed = layer_norm(middle[position].reshape(TOKENS, channels).astype(jnp.float32))
        for which in range(3):
            local[position, :, which] = (
                right_product(normed, matrix(4 + which))
                .astype(jnp.bfloat16)
                .reshape(frames, cells, width)
            )
        each(
            position,
            lambda s, g: transpose(local, received, qkv_send, qkv_recv, s, g, "start"),
        )

    order = sorted(
        range(per_device),
        key=lambda r: max((r - frames) % per_device, (r + frames) % per_device),
    )
    attended, finished = [], []
    for position in order:
        attended.append((position, attend(position)))
        if len(attended) > 1:
            earlier, sent = attended[-2]
            finished.append((earlier, finish(earlier, sent)))
        if len(finished) > 1:
            share_frames(*finished[-2])
    last, sent = attended[-1]
    finished.append((last, finish(last, sent)))
    for entry in finished[max(len(finished) - 2, 0) :]:
        share_frames(*entry)
    tokens_in = frames * cells
    row_cell = lax.rem(lax.broadcasted_iota(jnp.int32, (tokens_in, tokens_in), 0), cells)
    column_cell = lax.rem(lax.broadcasted_iota(jnp.int32, (tokens_in, tokens_in), 1), cells)
    keep = row_cell == column_cell
    for slot in range(per_device):
        each(slot, lambda s, g: landed(local, received, qkv_recv, s, g))
        queries, keys, values = (
            received[slot, :, which].reshape(tokens_in, width) for which in range(3)
        )
        result = masked_attention(queries, keys, values, keep, mixture)
        mixed[slot] = result.reshape(frames, cells, width)
        each(slot, lambda s, g: transpose(mixed, returned, mix_send, mix_recv, s, g, "start"))
    sent = []
    for slot in range(per_device):
        each(slot, lambda s, g: landed(mixed, returned, mix_recv, s, g))
        total = jnp.dot(
            returned[slot].reshape(TOKENS, width), matrix(7), preferred_element_type=jnp.float32
        )
        time_part[slot] = total.astype(jnp.bfloat16).reshape(tiles, rows, channels)
        sent.append(scatter(me, tile, tiles, slot, time_part, time_arrived, rt_send, rt_recv))
    for slot in range(per_device):
        total = gather_sum(tile, tiles, slot, time_part, time_arrived, sent[slot])
        own = middle[slot, tile].astype(jnp.float32) + total
        out_ref[slot] = own.astype(jnp.bfloat16)
    for slot in range(per_device):
        each(slot, lambda s, g: transpose(local, received, qkv_send, qkv_recv, s, g, "wait"))
        each(slot, lambda s, g: transpose(mixed, returned, mix_send, mix_recv, s, g, "wait"))


    for copy in copies.values():
        copy.wait_send()


def whole_block(cycle, tiles, lists, counts, latents, gain, shift, conv_weight, *matrices):
    per_device, rows, channels = latents.shape
    taps, width = conv_weight.shape[:2]
    frames = per_device * cycle // CAMS
    cells = TOKENS // frames
    kind = jnp.bfloat16
    dma = pltpu.SemaphoreType.DMA
    by_tile = dma((per_device, tiles))
    by_frame = dma((per_device, frames))
    vmem = pl.BlockSpec(memory_space=pltpu.VMEM)
    smem = pl.BlockSpec(memory_space=pltpu.SMEM)
    shares = pltpu.VMEM((per_device, tiles, rows, channels), kind)
    patches = pltpu.VMEM((per_device, 2, P_SIZE, 2, PATCH, width), kind)
    return pl.pallas_call(
        functools.partial(block_kernel, cycle, tiles),
        out_shape=jax.ShapeDtypeStruct((per_device, rows, channels), kind),
        in_specs=[smem] * 2 + [vmem] * 3 + [pl.BlockSpec(memory_space=pl.ANY)] * 9,
        out_specs=vmem,
        scratch_shapes=[
            shares,
            pltpu.VMEM((taps, TOKENS, channels), kind),
            pltpu.VMEM((taps, width, channels), kind),
            pltpu.VMEM((per_device, tiles, TOKENS, width), kind),
            pltpu.VMEM((TOKENS, width), jnp.float32),
            pltpu.VMEM((8, width, channels), kind),
            pltpu.VMEM((per_device, TOKENS, width), kind),
            pltpu.VMEM((per_device, NPATCH, 2, PATCH, width), kind),
            patches,
            patches,
            shares,
            shares,
            pltpu.VMEM((TOKENS, width), jnp.float32),
            shares,
            pltpu.VMEM((per_device, frames, 3, cells, width), kind),
            pltpu.VMEM((per_device, frames, 3, cells, width), kind),
            pltpu.VMEM((per_device, frames, cells, width), kind),
            pltpu.VMEM((per_device, frames, cells, width), kind),
            shares,
            shares,
            dma((taps,)),
            dma((8,)),
            by_tile, by_tile, by_tile, by_tile,
            dma((per_device, 2)),
            dma((per_device, 2)),
            by_tile, by_tile, by_tile, by_tile,
            by_frame, by_frame, by_frame, by_frame,
            by_tile, by_tile,
        ],
        compiler_params=pltpu.CompilerParams(
            collective_id=1, has_side_effects=True, vmem_limit_bytes=VMEM_BYTES
        ),
        name="whole_block",
    )(lists, counts, latents, gain, shift, conv_weight, *matrices)


def on_device(
    latents, norm_gain, norm_shift, conv_weight,
    cross_query, cross_key, cross_value, cross_out,
    time_query, time_key, time_value, time_out,
    patch_lists, patch_counts,
):
    per_device, share_rows, _, channels = latents.shape
    blended = whole_block(
        lax.axis_size("camframe"), lax.axis_size("tile"), patch_lists, patch_counts,
        latents.reshape(per_device, share_rows * WW, channels),
        norm_gain, norm_shift, conv_weight.reshape(9, -1, channels),
        cross_query, cross_key, cross_value, cross_out,
        time_query, time_key, time_value, time_out,
    )
    return blended.reshape(latents.shape)


def solution(mesh):
    return jax.shard_map(
        on_device,
        mesh=mesh,
        in_specs=(
            P("camframe", "tile", None, None),
            P(),
            P(),
            P(None, None, "tile", None),
            P("tile", None),
            P("tile", None),
            P("tile", None),
            P("tile", None),
            P("tile", None),
            P("tile", None),
            P("tile", None),
            P("tile", None),
            P(),
            P(),
        ),
        out_specs=P("camframe", "tile", None, None),
        check_vma=False,
    )
```

time: 148 us -> 109 us (0.74)
  blocking collectives: 31.8 us -> 0 us
  matrix products: 21.1 us -> 0 us
  Pallas kernels: 89 us -> 105 us
    all_gather x2 -> x0, blocking collectives: 31.8 us -> none  [the longest x1 16.9 us: on_device(): hidden = lax.all_gather(own_hidden, 'tile', axis=3, tiled=True)]
    conv_general_dilated x1 -> x0, matrix products: 21.1 us -> none  [convolve(): lax.conv_general_dilated(activated, weight, (1, 1), ((1, 1), (1, 1)), dim...]
    pallas_call x2 -> x1, Pallas kernels: 89 us -> 105 us  [whole_block(): pl.pallas_call(functools.partial(block_kernel, cycle, tiles), out_shape=j...]
    unnamed x24 -> x3, local copies, waits for them, and re-layouts: 3.44 us -> 4.55 us
where the time goes in v3:
time: 109 us
  Pallas kernels  105 us (96%)
  local copies, waits for them, and re-layouts  4.55 us (4%)
    pallas_call x1, Pallas kernels, whole_block(): pl.pallas_call(functools.partial(block_kernel, cycle, tiles), out_shape=j...  105 us
    unnamed x3, local copies, waits for them, and re-layouts  4.55 us

profile of v3, /device:TPU:0, one launch (start us, length us, event | category | flops | bytes accessed | tf_op | source)
XLA Modules:
  0.0 109.2 jit_solution(16219301775187932764)
XLA Ops:
  0.0 1.4 %copy.16.counts_ref = s32[6,2]{1,0:T(8,128)} copy(s32[6,2]{0,1:T(2,128)} %param.27) | data formatting | bytes 96 | tf_op args[13]
  1.4 1.4 %copy.15.lists_ref = s32[6,2,2]{2,1,0:T(2,128)} copy(s32[6,2,2]{0,2,1:T(2,128)} %param.26) | data formatting | bytes 192 | tf_op args[12]
  2.7 104.7 %whole_block.1 = bf16[3,64,1280]{2,1,0:T(8,128)(2,1)} custom-call(s32[6,2,2]{2,1,0:T(2,128)} %copy.15.lists_ref, s32[6,2]{1,0:T(8,128)} %copy.16.counts_ref, bf16[3,64,1280]{2,1,0:T(8,128)(2,1)} %bitcast.5, f32[1280]{0:T(1024)} %gain_ref.1, f32[1280]{0:T(1024)} %shift_ref.1, bf16[9,640,1280]{2,1,0:T(8,128)(2,1)} %bitcast.3, bf16[640,1280]{1,0:T(8,128)(2,1)} %cq_ref.1, ...), custom_call_target="tpu_custom_call" | custom-call | tf_op jit(solution)/shard_map/whole_block/pallas_call | solution.py:456
  107.4 1.8 %copy.18 = bf16[3,8,8,1280]{3,2,1,0:T(8,128)(2,1)} copy(bf16[3,8,8,1280]{3,2,1,0:T(8,128)(2,1)} %bitcast.4) | data formatting | bytes 983040

commit v4 on v3

--- a/solution.py
+++ b/solution.py
@@ -19,7 +19,7 @@
 
 EPSILON = 1e-05
 MESH = pl.DeviceIdType.MESH
-VMEM_BYTES = 58 * 1024 * 1024
+VMEM_BYTES = 50 * 1024 * 1024
 
 
 def right_product(left, weight):

time: 109 us -> 110 us (level)
  Pallas kernels: 105 us -> 103 us
  local copies, waits for them, and re-layouts: 4.55 us -> 6.17 us
    unnamed x3 -> x11, local copies, waits for them, and re-layouts: 4.55 us -> 6.17 us
    pallas_call x1, Pallas kernels: 105 us -> 103 us  [whole_block(): pl.pallas_call(functools.partial(block_kernel, cycle, tiles), out_shape=j...]
where the time goes in v4:
time: 110 us
  Pallas kernels  103 us (94%)
  local copies, waits for them, and re-layouts  6.17 us (6%)
    pallas_call x1, Pallas kernels, whole_block(): pl.pallas_call(functools.partial(block_kernel, cycle, tiles), out_shape=j...  103 us
    unnamed x11, local copies, waits for them, and re-layouts  6.17 us

profile of v4, /device:TPU:0, one launch (start us, length us, event | category | flops | bytes accessed | tf_op | source)
XLA Modules:
  0.0 109.6 jit_solution(12496747531317955411)
XLA Ops:
  0.0 0.8 copy.16.counts_ref
  0.8 0.8 copy.15.lists_ref
  1.5 0.0 copy-start
  1.5 1.4 %copy-done = bf16[640,1280]{1,0:T(8,128)(2,1)S(1)} copy-done((bf16[640,1280]{1,0:T(8,128)(2,1)S(1)}, bf16[640,1280]{1,0:T(8,128)(2,1)}, u32[]{:S(2)}) %copy-start) | copy-done | bytes 1638424
  3.0 0.0 copy-start.1
  3.0 1.0 copy-done.1
  4.0 0.0 copy-start.2
  4.0 0.7 copy-done.2
  4.7 0.0 copy-start.3
  4.7 0.7 copy-done.3
  5.4 103.4 %whole_block.1 = bf16[3,64,1280]{2,1,0:T(8,128)(2,1)S(1)} custom-call(s32[6,2,2]{2,1,0:T(2,128)S(1)} %copy.15.lists_ref, s32[6,2]{1,0:T(8,128)S(1)} %copy.16.counts_ref, bf16[3,64,1280]{2,1,0:T(8,128)(2,1)S(1)} %bitcast.4, f32[1280]{0:T(1024)S(1)} %copy-done.2, f32[1280]{0:T(1024)S(1)} %copy-done.3, bf16[9,640,1280]{2,1,0:T(8,128)(2,1)} %bitcast.5, ...), custom_call_target="tpu_custom_call" | custom-call | tf_op jit(solution)/shard_map/whole_block/pallas_call | solution.py:456
  108.8 0.8 copy.18
Async XLA Ops:
  1.5 1.4 %copy-start = (bf16[640,1280]{1,0:T(8,128)(2,1)S(1)}, bf16[640,1280]{1,0:T(8,128)(2,1)}, u32[]{:S(2)}) copy-start(bf16[640,1280]{1,0:T(8,128)(2,1)} %cq_ref.1) | copy-start | bytes 4915204
  3.0 1.0 copy-start.1
  4.0 0.7 copy-start.2
  4.7 0.7 copy-start.3
